TPU v7x, 256 devices: a whole 4x4x8 slice. The times are simulated.
256 devices in a mesh: fac: 64 (over y, x_lo, z), chan: 4 (over x_hi, core).
Axes of the slice: x: 4 (x_hi: 2, x_lo: 2; x = x_hi * 2 + x_lo), y: 4, z: 8, core: 2. Of those that a mesh axis runs over, the one named last changes fastest.
Arguments:
- primal_image: float32 [64, 1024, 2048], P('chan', 'fac'), may hold values from 0 to 1
- dual_coef: float32 [4, 64, 512, 1024], P(None, 'chan', 'fac'), may hold values from -6 to 6
- l21_weight: float32 [4, 512, 1024], P(None, 'fac'), may hold values from 2 to 16
- visibilities: bfloat16 [64, 16384], P('fac', 'chan'), may hold values from -6 to 6
- tile_index: int32 [64, 16384], P('fac', 'chan'), may hold values from 0 to 4095
- kernel_values: bfloat16 [64, 16384, 128], P('fac', 'chan'), may hold values from -6 to 6
- kernel_pattern: int32 [64, 16384, 128], P('fac', 'chan'), may hold values 0 or 1
Outputs:
- image_next: float32 [64, 1024, 2048], P('chan', 'fac')
- dual_next: float32 [4, 64, 512, 1024], P(None, 'chan', 'fac')
All inputs are finite; a program needn't handle non-finite values. No bound on the sum of `kernel_pattern` on one device may be relied on, other than what follows from the above.
Results may differ from a plain program's by a relative error of at most 0.00035.
Values sent between devices are 32-bit elements; how exact they have to be, the bound alone decides.
No kernel may reach another device: no remote copies, remote signals or barrier semaphores. Data moves between devices by JAX's collectives and lax.ppermute only.
A program may use at most 128 MiB of HBM per device.

v0:
```python
import jax
import jax.numpy as jnp
import ml_dtypes
import numpy as np
from jax import lax
from jax.experimental import pallas as pl
from jax.experimental.pallas import tpu as pltpu
from jax.sharding import PartitionSpec as P

FILTER_LOW = [
    0.23037781330885523,
    0.7148465705525415,
    0.6308807679295904,
    -0.02798376941698385,
    -0.18703481171888114,
    0.030841381835986965,
    0.032883011666982945,
    -0.010597401784997278,
]
FILTER_HIGH = [(-1.0) ** offset * FILTER_LOW[7 - offset] for offset in range(8)]
STEP_PRIMAL = 0.5
STEP_DUAL = 1.0
LANES = 128
VMEM_BYTES = 48 * 1024 * 1024


def taps(filters, offset):
    table = np.asarray(filters, np.float64)
    valid = (offset >= 0) & (offset < 8)
    return np.where(valid, table[np.clip(offset, 0, 7)], 0.0)


def split_constant(matrix):
    matrix = matrix.astype(np.float32)
    high = matrix.astype(ml_dtypes.bfloat16)
    low = (matrix - high.astype(np.float32)).astype(ml_dtypes.bfloat16)
    return jnp.asarray(np.stack([high, low]))


def split(values):
    high = values.astype(jnp.bfloat16)
    low = (values - high.astype(jnp.float32)).astype(jnp.bfloat16)
    return high, low


def product(a, b):
    return jnp.dot(a, b, preferred_element_type=jnp.float32)


def product_left(matrix, values):
    high, low = split(values)
    return product(matrix[0], high) + product(matrix[0], low) + product(matrix[1], high)


def synthesis_rows(channels, rows):
    halves = rows // 2
    pixel = np.arange(rows)[:, None]
    blocks = []
    for first, count in ((0, halves), (-2, 2), (halves, 2)):
        coef = first + np.arange(count)[None, :]
        for filters in (FILTER_LOW, FILTER_HIGH):
            blocks.append(np.kron(np.eye(channels), taps(filters, pixel - 2 * coef + 3)))
    own_low, own_high, top_low, top_high, bottom_low, bottom_high = blocks
    return np.concatenate([own_low, own_high, top_low, bottom_low, top_high, bottom_high], axis=1)


def synthesis_columns():
    coef = np.arange(3 * LANES)[:, None] - LANES
    pixel = np.arange(2 * LANES)[None, :]
    return np.concatenate(
        [taps(filters, pixel - 2 * coef + 3) for filters in (FILTER_LOW, FILTER_HIGH)], axis=0
    )


def analysis_rows(channels, rows):
    coef = np.arange(rows // 2)[:, None]
    own, halo = [], []
    for filters in (FILTER_LOW, FILTER_HIGH):
        pixel = np.arange(rows)[None, :]
        own.append(np.kron(np.eye(channels), taps(filters, pixel - 2 * coef + 3)))
        sides = []
        for pixel_at in (-3, -2, -1, rows, rows + 1, rows + 2):
            column = taps(filters, pixel_at - 2 * coef + 3)
            sides.append(np.kron(np.eye(channels), column))
        halo.append(np.concatenate(sides, axis=1))
    return np.concatenate(own, axis=0), np.concatenate(halo, axis=0)


def analysis_columns():
    pixel = np.arange(4 * LANES)[:, None] - LANES
    coef = np.arange(LANES)[None, :]
    return np.concatenate(
        [taps(filters, pixel - 2 * coef + 3) for filters in (FILTER_LOW, FILTER_HIGH)], axis=1
    )


def border_rows(channels, rows):
    ends = (0, 1, 2, rows - 3, rows - 2, rows - 1)
    picked = [np.kron(np.eye(channels), np.arange(rows)[None, :] == row) for row in ends]
    return np.concatenate(picked, axis=0).astype(ml_dtypes.bfloat16)


def back_kernel(vis_ref, tile_ref, kernel_ref, pattern_ref, out_ref, cells_ref):
    count = tile_ref.shape[1]
    rows_here = out_ref.shape[0]
    step = 512

    @pl.when(pl.program_id(0) == 0)
    def _():
        def fill(index, carry):
            at = pl.multiple_of(index * step, step)
            tile = tile_ref[:, pl.ds(at, step)] & 3
            lane_tile = jnp.transpose(jnp.broadcast_to(tile, (LANES, step)))
            kept = jnp.where(pattern_ref[pl.ds(at, step), :] != 0, lane_tile, 4)
            values = kernel_ref[pl.ds(at, step), :].astype(jnp.float32)
            for part in range(4):
                cells_ref[pl.ds(at, step), part * LANES : (part + 1) * LANES] = jnp.where(
                    kept == part, values, 0.0
                ).astype(jnp.bfloat16)
            return carry

        lax.fori_loop(0, count // step, fill, 0)

    row = pl.program_id(0) * rows_here + lax.broadcasted_iota(jnp.int32, (rows_here, step), 0)

    def add(index, total):
        at = pl.multiple_of(index * step, step)
        here = (tile_ref[:, pl.ds(at, step)] >> 2) == row
        values = vis_ref[:, pl.ds(at, step)].astype(jnp.float32)
        spread = jnp.where(here, values, 0.0).astype(jnp.bfloat16)
        out_ref[...] += product(spread, cells_ref[pl.ds(at, step), :])
        return total

    out_ref[...] = jnp.zeros_like(out_ref)
    lax.fori_loop(0, count // step, add, 0)


def back_project(vis, tile, kernels, pattern, rows_all, quarter):
    count = tile.shape[1]
    block = 256
    whole = lambda i: (0, 0)
    return pl.pallas_call(
        back_kernel,
        grid=(rows_all // block,),
        in_specs=[
            pl.BlockSpec((1, count), whole),
            pl.BlockSpec((1, count), whole),
            pl.BlockSpec((count, LANES), whole),
            pl.BlockSpec((count, LANES), whole),
        ],
        out_specs=pl.BlockSpec((block, quarter), lambda i: (i, 0)),
        out_shape=jax.ShapeDtypeStruct((rows_all, quarter), jnp.float32),
        scratch_shapes=[pltpu.VMEM((count, quarter), jnp.bfloat16)],
        compiler_params=pltpu.CompilerParams(vmem_limit_bytes=VMEM_BYTES),
        cost_estimate=pl.CostEstimate(
            flops=2 * rows_all * count * quarter, bytes_accessed=6 << 20, transcendentals=0
        ),
        name="back_project",
    )(vis, tile, kernels, pattern)


def synthesis_kernel(dual_ref, top_ref, bottom_ref, primal_ref, rows_ref, columns_ref, out_ref, mid_ref):
    tiles = dual_ref.shape[2] // LANES
    for kind in range(2):
        for at in range(0, tiles, 2):
            lanes = slice(at * LANES, (at + 2) * LANES)
            stacked = jnp.concatenate(
                [
                    dual_ref[kind, :, lanes],
                    dual_ref[kind + 2, :, lanes],
                    top_ref[kind, :, lanes],
                    bottom_ref[kind, :, lanes],
                    top_ref[kind + 2, :, lanes],
                    bottom_ref[kind + 2, :, lanes],
                ],
                axis=0,
            )
            high, low = split(product_left(rows_ref, stacked))
            mid_ref[kind, 0, :, lanes] = high
            mid_ref[kind, 1, :, lanes] = low
    for at in range(tiles):
        first, last = max(at - 1, 0), min(at + 2, tiles)
        lanes = slice(first * LANES, last * LANES)
        total = 0.0
        for kind in range(2):
            base = (3 * kind + first - at + 1) * LANES
            part = slice(base, base + (last - first) * LANES)
            total = total + product(mid_ref[kind, 0, :, lanes], columns_ref[0, part, :])
            total = total + product(mid_ref[kind, 1, :, lanes], columns_ref[0, part, :])
            total = total + product(mid_ref[kind, 0, :, lanes], columns_ref[1, part, :])
        pixels = slice(2 * at * LANES, 2 * (at + 1) * LANES)
        out_ref[:, pixels] = primal_ref[:, pixels] - STEP_PRIMAL * total


def synthesize(dual, top, bottom, primal, channels, rows):
    pixels, columns = primal.shape
    return pl.pallas_call(
        synthesis_kernel,
        out_shape=jax.ShapeDtypeStruct(primal.shape, jnp.float32),
        scratch_shapes=[pltpu.VMEM((2, 2, pixels, columns // 2), jnp.bfloat16)],
        compiler_params=pltpu.CompilerParams(vmem_limit_bytes=VMEM_BYTES),
        cost_estimate=pl.CostEstimate(
            flops=4 << 30, bytes_accessed=8 << 20, transcendentals=0
        ),
        name="synthesis",
    )(
        dual,
        top,
        bottom,
        primal,
        split_constant(synthesis_rows(channels, rows)),
        split_constant(synthesis_columns()),
    )


def image_kernel(base_ref, back_ref, primal_ref, pick_ref, image_ref, top_ref, bottom_ref):
    image = jnp.maximum(base_ref[...] - STEP_PRIMAL * back_ref[0], 0.0)
    image_ref[...] = image
    high, low = split(2.0 * image - primal_ref[...])
    sides = product(pick_ref[...], high) + product(pick_ref[...], low)
    half = sides.shape[0] // 2
    top_ref[...] = sides[:half]
    bottom_ref[...] = sides[half:]


def update_image(base, back, primal, channels, rows):
    parts, pixels, quarter = back.shape
    block = pl.BlockSpec((pixels, quarter), lambda i: (0, i))
    side = pl.BlockSpec((3 * channels, quarter), lambda i: (0, i))
    side_shape = jax.ShapeDtypeStruct((3 * channels, parts * quarter), jnp.float32)
    pick = border_rows(channels, rows)
    return pl.pallas_call(
        image_kernel,
        grid=(parts,),
        in_specs=[
            block,
            pl.BlockSpec((1, pixels, quarter), lambda i: (i, 0, 0)),
            block,
            pl.BlockSpec(pick.shape, lambda i: (0, 0)),
        ],
        out_specs=[block, side, side],
        out_shape=[jax.ShapeDtypeStruct(base.shape, jnp.float32), side_shape, side_shape],
        compiler_params=pltpu.CompilerParams(vmem_limit_bytes=VMEM_BYTES),
        cost_estimate=pl.CostEstimate(flops=4 << 20, bytes_accessed=8 << 20, transcendentals=0),
        name="update_image",
    )(base, back, primal, jnp.asarray(pick))


def analysis_kernel(
    image_ref, primal_ref, above_ref, below_ref, dual_ref, own_ref, halo_ref, columns_ref,
    update_ref, squares_ref, mid_ref,
):
    tiles = image_ref.shape[1] // LANES
    half = mid_ref.shape[1] // 2
    for at in range(0, tiles, 2):
        lanes = slice(at * LANES, (at + 2) * LANES)
        change = 2.0 * image_ref[:, lanes] - primal_ref[:, lanes]
        sides = jnp.concatenate([above_ref[:, lanes], below_ref[:, lanes]], axis=0)
        banded = product_left(own_ref, change) + product_left(halo_ref, sides)
        high, low = split(banded)
        mid_ref[0, :, lanes] = high
        mid_ref[1, :, lanes] = low
    for at in range(0, tiles, 2):
        first, last = max(at - 1, 0), min(at + 3, tiles)
        lanes = slice(first * LANES, last * LANES)
        part = slice((first - at + 1) * LANES, (last - at + 1) * LANES)
        both = product(mid_ref[0, :, lanes], columns_ref[0, part, :])
        both = both + product(mid_ref[1, :, lanes], columns_ref[0, part, :])
        both = both + product(mid_ref[0, :, lanes], columns_ref[1, part, :])
        out = slice(at // 2 * LANES, (at // 2 + 1) * LANES)
        for band in range(4):
            rows = slice(band // 2 * half, (band // 2 + 1) * half)
            cols = slice(band % 2 * LANES, (band % 2 + 1) * LANES)
            update = dual_ref[band, :, out] + STEP_DUAL * both[rows, cols]
            update_ref[band, :, out] = update
            squares = update * update
            squares_ref[band, :, out] = jnp.sum(
                squares.reshape(-1, squares_ref.shape[1], LANES), axis=0
            )


def analyze(image, primal, above, below, dual, channels, rows):
    own, halo = analysis_rows(channels, rows)
    return pl.pallas_call(
        analysis_kernel,
        out_shape=[
            jax.ShapeDtypeStruct(dual.shape, jnp.float32),
            jax.ShapeDtypeStruct((4, rows // 2, dual.shape[2]), jnp.float32),
        ],
        scratch_shapes=[pltpu.VMEM((2,) + image.shape, jnp.bfloat16)],
        compiler_params=pltpu.CompilerParams(vmem_limit_bytes=VMEM_BYTES),
        cost_estimate=pl.CostEstimate(flops=4 << 30, bytes_accessed=10 << 20, transcendentals=0),
        name="analysis",
    )(
        image,
        primal,
        above,
        below,
        dual,
        split_constant(own),
        split_constant(halo),
        split_constant(analysis_columns()),
    )


def project_kernel(update_ref, weight_ref, one_ref, two_ref, three_ref, four_ref, out_ref):
    total = (one_ref[0] + two_ref[0]) + (three_ref[0] + four_ref[0])
    weight = weight_ref[0]
    factor = weight / jnp.maximum(jnp.sqrt(total), weight)
    count = factor.shape[0]
    for channel in range(update_ref.shape[1] // count):
        rows = slice(channel * count, (channel + 1) * count)
        out_ref[0, rows, :] = update_ref[0, rows, :] * factor


def project(update, weight, sums):
    bands, pixels, columns = update.shape
    wide = pl.BlockSpec((1, pixels, columns), lambda i: (i, 0, 0))
    narrow = pl.BlockSpec((1, weight.shape[1], columns), lambda i: (i, 0, 0))
    return pl.pallas_call(
        project_kernel,
        grid=(bands,),
        in_specs=[wide] + [narrow] * 5,
        out_specs=wide,
        out_shape=jax.ShapeDtypeStruct(update.shape, jnp.float32),
        compiler_params=pltpu.CompilerParams(vmem_limit_bytes=VMEM_BYTES),
        cost_estimate=pl.CostEstimate(flops=4 << 20, bytes_accessed=5 << 20, transcendentals=0),
        name="project",
    )(update, weight, *sums)


def shards(
    primal_image, dual_coef, l21_weight, visibilities, tile_index, kernel_values, kernel_pattern
):
    facets, groups = lax.axis_size("fac"), lax.axis_size("chan")
    channels, rows, columns = primal_image.shape
    quarter = columns // groups
    forward = [(i, i + 1) for i in range(facets - 1)]
    backward = [(b, a) for a, b in forward]

    halves = rows // 2
    top = lax.ppermute(
        dual_coef[:, :, halves - 2 :].reshape(4, 2 * channels, columns // 2), "fac", forward
    )
    bottom = lax.ppermute(
        dual_coef[:, :, :2].reshape(4, 2 * channels, columns // 2), "fac", backward
    )

    gridded = back_project(
        visibilities, tile_index, kernel_values[0], kernel_pattern[0], rows * facets, quarter
    )
    by_facet = lax.all_to_all(
        gridded.reshape(facets, rows, quarter), "fac", split_axis=0, concat_axis=0, tiled=True
    )
    back = lax.all_to_all(by_facet, "chan", split_axis=0, concat_axis=0, tiled=True)
    back = back.reshape(groups, channels * rows, quarter)

    primal = primal_image.reshape(channels * rows, columns)
    dual = dual_coef.reshape(4, channels * halves, columns // 2)
    base = synthesize(dual, top, bottom, primal, channels, rows)
    image, first, last = update_image(base, back, primal, channels, rows)
    above = lax.ppermute(last, "fac", forward)
    below = lax.ppermute(first, "fac", backward)
    update, squares = analyze(image, primal, above, below, dual, channels, rows)
    sums = [squares]
    for step in range(1, groups):
        pairs = [(i, (i + step) % groups) for i in range(groups)]
        sums.append(lax.ppermute(squares, "chan", pairs))
    dual_next = project(update, l21_weight, sums)
    return (image.reshape(primal_image.shape), dual_next.reshape(dual_coef.shape))


def solution(mesh):
    in_specs = (
        P("chan", "fac", None),
        P(None, "chan", "fac", None),
        P(None, "fac", None),
        P("fac", "chan"),
        P("fac", "chan"),
        P("fac", "chan", None),
        P("fac", "chan", None),
    )
    out_specs = (P("chan", "fac", None), P(None, "chan", "fac", None))
    return jax.shard_map(shards, mesh=mesh, in_specs=in_specs, out_specs=out_specs, check_vma=False)
```

profile of v0, /device:TPU:8, one launch (start us, length us, event | category | flops | bytes accessed | tf_op | source)
XLA Modules:
  0.0 163.0 jit_solution(9594428614310150661)
XLA Ops:
  0.6 0.0 copy-start.4
  0.6 1.6 copy-done.4
  2.2 0.0 copy-start.6
  2.2 1.2 copy-done.6
  3.4 0.0 copy-start.7
  3.5 0.7 copy-done.7
  4.2 0.0 copy-start.8
  4.2 0.7 copy-done.8
  4.9 11.6 %back_project.1 = f32[1024,512]{1,0:T(8,128)S(1)} custom-call(bf16[1,4096]{1,0:T(2,128)(2,1)S(1)} %copy-done.7, s32[1,4096]{1,0:T(1,128)S(1)} %copy-done.8, bf16[4096,128]{1,0:T(8,128)(2,1)S(1)} %bitcast.14, s32[4096,128]{1,0:T(8,128)S(1)} %bitcast.12), custom_call_target="tpu_custom_call" | custom-call | flops 4294967296 | bytes 6291456 | tf_op jit(solution)/shard_map/back_project/pallas_call | solution.py:142
  16.5 63.5 %all_to_all.10 = f32[64,16,512]{2,1,0:T(8,128)} all-to-all(f32[64,16,512]{2,1,0:T(8,128)S(1)} %bitcast.11), channel_id=1, replica_groups=mesh['fac'=64,'chan'=4] {'fac'}, dimensions={0} | all-to-all | bytes 4194304 | tf_op jit(solution)/shard_map/all_to_all | solution.py:352
  80.0 4.0 %all-to-all-start.1 = ((f32[64,16,512]{2,1,0:T(8,128)}), f32[64,16,512]{2,1,0:T(8,128)S(1)}, u32[]{:S(2)}, u32[]{:S(2)}) async-start(f32[64,16,512]{2,1,0:T(8,128)} %all_to_all.10), calls=%async_computation.1 | async-start | bytes 4194304 | tf_op jit(solution)/shard_map/all_to_all | solution.py:355
  84.0 2.8 %fusion = (f32[4,16,2,1024]{3,2,1,0:T(2,128)S(1)}, f32[4,16,2,1024]{3,2,1,0:T(2,128)S(1)}) fusion(f32[4,16,8,1024]{3,2,1,0:T(8,128)} %param.14), kind=kLoop, calls=%fused_computation | loop fusion | bytes 2097152 | tf_op jit(solution)/shard_map/slice | solution.py:346
  86.8 0.0 copy-start.9
  86.8 0.0 copy-start.11
  86.8 0.3 copy.15
  87.1 0.3 copy.16
  87.4 3.3 %collective-permute-start = (f32[4,32,1024]{2,1,0:T(8,128)S(1)}, f32[4,32,1024]{2,1,0:T(8,128)S(1)}, u32[]{:S(2)}, u32[]{:S(2)}) collective-permute-start(f32[4,32,1024]{2,1,0:T(8,128)S(1)} %copy.16), channel_id=1, source_target_pairs={{0,4},{4,8},{8,12},{12,16},{16,20},{20,24},{24,28},{28,32},{32,36}... | collective-permute-start | bytes 1572872 | tf_op jit(solution)/shard_map/ppermute | solution.py:342
  90.7 0.3 copy.17
  91.1 0.3 copy.18
  91.4 5.6 %collective-permute-start.1 = (f32[4,32,1024]{2,1,0:T(8,128)S(1)}, f32[4,32,1024]{2,1,0:T(8,128)S(1)}, u32[]{:S(2)}, u32[]{:S(2)}) collective-permute-start(f32[4,32,1024]{2,1,0:T(8,128)S(1)} %copy.18), channel_id=1, source_target_pairs={{4,0},{8,4},{12,8},{16,12},{20,16},{24,20},{28,24},{32,28},{36,32}... | collective-permute-start | bytes 1572872 | tf_op jit(solution)/shard_map/ppermute | solution.py:345
  97.0 9.8 %collective-permute-done.top_ref = f32[4,32,1024]{2,1,0:T(8,128)S(1)} collective-permute-done((f32[4,32,1024]{2,1,0:T(8,128)S(1)}, f32[4,32,1024]{2,1,0:T(8,128)S(1)}, u32[]{:S(2)}, u32[]{:S(2)}) %collective-permute-start) | collective-permute-done | bytes 524320 | tf_op jit(solution)/shard_map/ppermute | solution.py:342
  106.8 1.8 %collective-permute-done.1.bottom_ref = f32[4,32,1024]{2,1,0:T(8,128)S(1)} collective-permute-done((f32[4,32,1024]{2,1,0:T(8,128)S(1)}, f32[4,32,1024]{2,1,0:T(8,128)S(1)}, u32[]{:S(2)}, u32[]{:S(2)}) %collective-permute-start.1) | collective-permute-done | bytes 524320 | tf_op jit(solution)/shard_map/ppermute | solution.py:345
  108.6 0.0 copy-done.9
  108.6 0.0 copy-done.11
  108.6 0.0 copy-start.3
  108.6 6.9 %synthesis.1.base_ref = f32[256,2048]{1,0:T(8,128)S(1)} custom-call(f32[4,128,1024]{2,1,0:T(8,128)} %bitcast.21, f32[4,32,1024]{2,1,0:T(8,128)S(1)} %collective-permute-done.top_ref, f32[4,32,1024]{2,1,0:T(8,128)S(1)} %collective-permute-done.1.bottom_ref, f32[256,2048]{1,0:T(8,128)} %bitcast.15, bf16[2,256,384]{2,1,0:T(8,128)(2,1)S(1)} %copy-done.11, ...), custom_call_target="tpu_custom_call" | custom-call | flops 4294967296 | bytes 8388608 | tf_op jit(solution)/shard_map/synthesis/pallas_call | solution.py:197
  115.5 0.0 copy-start
  115.5 1.3 copy-done
  116.8 5.6 %all-to-all-done.1 = f32[64,16,512]{2,1,0:T(8,128)S(1)} async-done(((f32[64,16,512]{2,1,0:T(8,128)}), f32[64,16,512]{2,1,0:T(8,128)S(1)}, u32[]{:S(2)}, u32[]{:S(2)}) %all-to-all-start.1) | async-done | bytes 2097184 | tf_op jit(solution)/shard_map/all_to_all | solution.py:355
  122.4 0.0 copy-done.3
  122.4 0.0 copy-start.1
  122.4 1.6 copy-done.1
  124.0 0.0 copy-start.10
  124.0 0.0 copy-start.12
  124.0 0.0 copy-start.13
  124.0 4.1 %update_image.1 = (f32[256,2048]{1,0:T(8,128)}, f32[48,2048]{1,0:T(8,128)S(1)}, f32[48,2048]{1,0:T(8,128)S(1)}) custom-call(f32[256,2048]{1,0:T(8,128)S(1)} %copy-done.1, f32[4,256,512]{2,1,0:T(8,128)S(1)} %bitcast.10, f32[256,2048]{1,0:T(8,128)} %bitcast.16, bf16[96,256]{1,0:T(8,128)(2,1)S(1)} %copy-done.3), custom_call_target="tpu_custom_call" | custom-call | flops 4194304 | bytes 8388608 | tf_op jit(solution)/shard_map/update_image/pallas_call | solution.py:232
  128.2 1.9 %collective-permute-start.2 = (f32[48,2048]{1,0:T(8,128)S(1)}, f32[48,2048]{1,0:T(8,128)S(1)}, u32[]{:S(2)}, u32[]{:S(2)}) collective-permute-start(f32[48,2048]{1,0:T(8,128)S(1)} %get-tuple-element.8), channel_id=1, source_target_pairs={{0,4},{4,8},{8,12},{12,16},{16,20},{20,24},{24,28},{28,32},{32,36}... | collective-permute-start | bytes 1179656 | tf_op jit(solution)/shard_map/ppermute | solution.py:362
  130.1 6.9 %collective-permute-start.3 = (f32[48,2048]{1,0:T(8,128)S(1)}, f32[48,2048]{1,0:T(8,128)S(1)}, u32[]{:S(2)}, u32[]{:S(2)}) collective-permute-start(f32[48,2048]{1,0:T(8,128)S(1)} %get-tuple-element.9), channel_id=1, source_target_pairs={{4,0},{8,4},{12,8},{16,12},{20,16},{24,20},{28,24},{32,28},{36,32}... | collective-permute-start | bytes 1179656 | tf_op jit(solution)/shard_map/ppermute | solution.py:363
  137.0 6.7 %collective-permute-done.2.above_ref = f32[48,2048]{1,0:T(8,128)S(1)} collective-permute-done((f32[48,2048]{1,0:T(8,128)S(1)}, f32[48,2048]{1,0:T(8,128)S(1)}, u32[]{:S(2)}, u32[]{:S(2)}) %collective-permute-start.2) | collective-permute-done | bytes 393248 | tf_op jit(solution)/shard_map/ppermute | solution.py:362
  143.7 1.2 collective-permute-done.3.below_ref
  144.9 0.0 copy-done.10
  144.9 0.0 copy-done.12
  144.9 0.0 copy-done.13
  144.9 0.0 copy-start.5
  144.9 1.6 copy-done.5
  146.5 0.0 copy-start.2
  146.5 5.8 %analysis.1 = (f32[4,128,1024]{2,1,0:T(8,128)S(1)}, f32[4,8,1024]{2,1,0:T(8,128)S(1)}) custom-call(f32[256,2048]{1,0:T(8,128)S(1)} %copy-done.5, f32[256,2048]{1,0:T(8,128)} %bitcast.17, f32[48,2048]{1,0:T(8,128)S(1)} %collective-permute-done.2.above_ref, f32[48,2048]{1,0:T(8,128)S(1)} %collective-permute-done.3.below_ref, f32[4,128,1024]{2,1,0:T(8,128)} %bitcast.22, ...), custom_call_target="tpu_custom_call" | custom-call | flops 4294967296 | bytes 10485760 | tf_op jit(solution)/shard_map/analysis/pallas_call | solution.py:284
  152.3 0.1 collective-permute-start.6
  152.3 1.6 collective-permute-start.5
  153.9 0.0 collective-permute-start.4
  153.9 2.1 %collective-permute-done.6.four_ref = f32[4,8,1024]{2,1,0:T(8,128)S(1)} collective-permute-done((f32[4,8,1024]{2,1,0:T(8,128)S(1)}, f32[4,8,1024]{2,1,0:T(8,128)S(1)}, u32[]{:S(2)}, u32[]{:S(2)}) %collective-permute-start.6) | collective-permute-done | bytes 131104 | tf_op jit(solution)/shard_map/ppermute | solution.py:368
  156.0 4.2 %collective-permute-done.5.three_ref = f32[4,8,1024]{2,1,0:T(8,128)S(1)} collective-permute-done((f32[4,8,1024]{2,1,0:T(8,128)S(1)}, f32[4,8,1024]{2,1,0:T(8,128)S(1)}, u32[]{:S(2)}, u32[]{:S(2)}) %collective-permute-start.5) | collective-permute-done | bytes 131104 | tf_op jit(solution)/shard_map/ppermute | solution.py:368
  160.2 0.9 collective-permute-done.4.two_ref
  161.2 0.0 copy-done.2
  161.2 1.9 %project.1 = f32[4,128,1024]{2,1,0:T(8,128)} custom-call(f32[4,128,1024]{2,1,0:T(8,128)S(1)} %get-tuple-element.10.update_ref, f32[4,8,1024]{2,1,0:T(8,128)S(1)} %copy-done.2, f32[4,8,1024]{2,1,0:T(8,128)S(1)} %get-tuple-element.11.one_ref, f32[4,8,1024]{2,1,0:T(8,128)S(1)} %collective-permute-done.4.two_ref, ...), custom_call_target="tpu_custom_call" | custom-call | flops 4194304 | bytes 5242880 | tf_op jit(solution)/shard_map/project/pallas_call | solution.py:320
Async XLA Ops:
  0.6 1.6 copy-start.4
  2.2 1.2 copy-start.6
  3.4 0.7 copy-start.7
  4.2 0.7 copy-start.8
  80.0 42.4 %all-to-all-start.1 = ((f32[64,16,512]{2,1,0:T(8,128)}), f32[64,16,512]{2,1,0:T(8,128)S(1)}, u32[]{:S(2)}, u32[]{:S(2)}) async-start(f32[64,16,512]{2,1,0:T(8,128)} %all_to_all.10), calls=%async_computation.1 | async-start | bytes 4194304 | tf_op jit(solution)/shard_map/all_to_all | solution.py:355
  86.8 21.8 %copy-start.9 = (bf16[2,768,256]{2,1,0:T(8,128)(2,1)S(1)}, bf16[2,768,256]{2,1,0:T(8,128)(2,1)}, u32[]{:S(2)}) copy-start(bf16[2,768,256]{2,1,0:T(8,128)(2,1)} %constant.13.clone.columns_ref) | copy-start | bytes 2359300
  86.8 21.8 %copy-start.11 = (bf16[2,256,384]{2,1,0:T(8,128)(2,1)S(1)}, bf16[2,256,384]{2,1,0:T(8,128)(2,1)}, u32[]{:S(2)}) copy-start(bf16[2,256,384]{2,1,0:T(8,128)(2,1)} %constant.12.clone.rows_ref) | copy-start | bytes 1179652
  87.4 19.3 %collective-permute-start = (f32[4,32,1024]{2,1,0:T(8,128)S(1)}, f32[4,32,1024]{2,1,0:T(8,128)S(1)}, u32[]{:S(2)}, u32[]{:S(2)}) collective-permute-start(f32[4,32,1024]{2,1,0:T(8,128)S(1)} %copy.16), channel_id=1, source_target_pairs={{0,4},{4,8},{8,12},{12,16},{16,20},{20,24},{24,28},{28,32},{32,36}... | collective-permute-start | bytes 1572872 | tf_op jit(solution)/shard_map/ppermute | solution.py:342
  91.4 17.2 %collective-permute-start.1 = (f32[4,32,1024]{2,1,0:T(8,128)S(1)}, f32[4,32,1024]{2,1,0:T(8,128)S(1)}, u32[]{:S(2)}, u32[]{:S(2)}) collective-permute-start(f32[4,32,1024]{2,1,0:T(8,128)S(1)} %copy.18), channel_id=1, source_target_pairs={{4,0},{8,4},{12,8},{16,12},{20,16},{24,20},{28,24},{32,28},{36,32}... | collective-permute-start | bytes 1572872 | tf_op jit(solution)/shard_map/ppermute | solution.py:345
  108.6 13.9 %copy-start.3 = (bf16[96,256]{1,0:T(8,128)(2,1)S(1)}, bf16[96,256]{1,0:T(8,128)(2,1)}, u32[]{:S(2)}) copy-start(bf16[96,256]{1,0:T(8,128)(2,1)} %constant.14.clone.pick_ref) | copy-start | bytes 147460
  115.5 1.3 copy-start
  122.4 1.6 copy-start.1
  124.0 20.9 %copy-start.10 = (bf16[2,512,256]{2,1,0:T(8,128)(2,1)S(1)}, bf16[2,512,256]{2,1,0:T(8,128)(2,1)}, u32[]{:S(2)}) copy-start(bf16[2,512,256]{2,1,0:T(8,128)(2,1)} %constant.17.clone.columns_ref) | copy-start | bytes 1572868
  124.0 20.9 %copy-start.12 = (bf16[2,256,256]{2,1,0:T(8,128)(2,1)S(1)}, bf16[2,256,256]{2,1,0:T(8,128)(2,1)}, u32[]{:S(2)}) copy-start(bf16[2,256,256]{2,1,0:T(8,128)(2,1)} %constant.15.clone.own_ref) | copy-start | bytes 786436
  124.0 20.9 %copy-start.13 = (bf16[2,256,96]{2,1,0:T(8,128)(2,1)S(1)}, bf16[2,256,96]{2,1,0:T(8,128)(2,1)}, u32[]{:S(2)}) copy-start(bf16[2,256,96]{2,1,0:T(8,128)(2,1)} %constant.16.clone.halo_ref) | copy-start | bytes 294916
  128.2 15.5 %collective-permute-start.2 = (f32[48,2048]{1,0:T(8,128)S(1)}, f32[48,2048]{1,0:T(8,128)S(1)}, u32[]{:S(2)}, u32[]{:S(2)}) collective-permute-start(f32[48,2048]{1,0:T(8,128)S(1)} %get-tuple-element.8), channel_id=1, source_target_pairs={{0,4},{4,8},{8,12},{12,16},{16,20},{20,24},{24,28},{28,32},{32,36}... | collective-permute-start | bytes 1179656 | tf_op jit(solution)/shard_map/ppermute | solution.py:362
  130.1 14.8 %collective-permute-start.3 = (f32[48,2048]{1,0:T(8,128)S(1)}, f32[48,2048]{1,0:T(8,128)S(1)}, u32[]{:S(2)}, u32[]{:S(2)}) collective-permute-start(f32[48,2048]{1,0:T(8,128)S(1)} %get-tuple-element.9), channel_id=1, source_target_pairs={{4,0},{8,4},{12,8},{16,12},{20,16},{24,20},{28,24},{32,28},{36,32}... | collective-permute-start | bytes 1179656 | tf_op jit(solution)/shard_map/ppermute | solution.py:363
  144.9 1.6 copy-start.5
  146.5 14.7 %copy-start.2 = (f32[4,8,1024]{2,1,0:T(8,128)S(1)}, f32[4,8,1024]{2,1,0:T(8,128)}, u32[]{:S(2)}) copy-start(f32[4,8,1024]{2,1,0:T(8,128)} %weight_ref.1) | copy-start | bytes 393220
  152.3 3.8 %collective-permute-start.6 = (f32[4,8,1024]{2,1,0:T(8,128)S(1)}, f32[4,8,1024]{2,1,0:T(8,128)S(1)}, u32[]{:S(2)}, u32[]{:S(2)}) collective-permute-start(f32[4,8,1024]{2,1,0:T(8,128)S(1)} %get-tuple-element.11.one_ref), channel_id=1, source_target_pairs={{0,3},{1,0},{2,1},{3,2},{4,7},{5,4},{6,5},{7,6},{8,11},{9,8},{10,9... | collective-permute-start | bytes 393224 | tf_op jit(solution)/shard_map/ppermute | solution.py:368
  152.3 7.9 %collective-permute-start.5 = (f32[4,8,1024]{2,1,0:T(8,128)S(1)}, f32[4,8,1024]{2,1,0:T(8,128)S(1)}, u32[]{:S(2)}, u32[]{:S(2)}) collective-permute-start(f32[4,8,1024]{2,1,0:T(8,128)S(1)} %get-tuple-element.11.one_ref), channel_id=1, source_target_pairs={{0,2},{1,3},{2,0},{3,1},{4,6},{5,7},{6,4},{7,5},{8,10},{9,11},{10,... | collective-permute-start | bytes 393224 | tf_op jit(solution)/shard_map/ppermute | solution.py:368
  153.9 7.3 %collective-permute-start.4 = (f32[4,8,1024]{2,1,0:T(8,128)S(1)}, f32[4,8,1024]{2,1,0:T(8,128)S(1)}, u32[]{:S(2)}, u32[]{:S(2)}) collective-permute-start(f32[4,8,1024]{2,1,0:T(8,128)S(1)} %get-tuple-element.11.one_ref), channel_id=1, source_target_pairs={{0,1},{1,2},{2,3},{3,0},{4,5},{5,6},{6,7},{7,4},{8,9},{9,10},{10,1... | collective-permute-start | bytes 393224 | tf_op jit(solution)/shard_map/ppermute | solution.py:368
where the time goes:
time: 164 us; the launch traced here: 163 us
  blocking collectives  63.5 us (39%)
  waiting for transfers between devices  32.4 us (20%)
  Pallas kernels  30.3 us (18%)
  starting transfers between devices  23.3 us (14%)
  local copies, waits for them, and re-layouts  12.8 us (8%)
    all_to_all x1, blocking collectives, shards(): lax.all_to_all(gridded.reshape(facets, rows, quarter), 'fac', split_axis=...  63.5 us
    pallas_call x1, Pallas kernels, back_project(): pl.pallas_call(back_kernel, grid=(rows_all // block,), in_specs=[pl.Block...  11.6 us
    ppermute x1, waiting for transfers between devices, shards(): lax.ppermute(dual_coef[:, :, halves - 2:].reshape(4, 2 * channels, column...  9.81 us
    unnamed x28, local copies, waits for them, and re-layouts  8.77 us
    ppermute x3, waiting for transfers between devices, shards(): sums.append(lax.ppermute(squares, 'chan', pairs))  7.26 us
    ppermute x1, starting transfers between devices, shards(): below = lax.ppermute(first, 'fac', backward)  6.93 us
    pallas_call x1, Pallas kernels, synthesize(): pl.pallas_call(synthesis_kernel, out_shape=jax.ShapeDtypeStruct(primal.sh...  6.9 us
    ppermute x1, waiting for transfers between devices, shards(): above = lax.ppermute(last, 'fac', forward)  6.69 us
  transfers between devices with their start and end apart: 8, of which 8 were waited for; matrix products, arithmetic and copies ran while one was open for 2% of the time, Pallas kernels for 4%

commit v1 on v0

v1 whole, which is shorter than its diff:
```python
import functools

import jax
import jax.numpy as jnp
import ml_dtypes
import numpy as np
from jax import lax
from jax.experimental import pallas as pl
from jax.experimental.pallas import tpu as pltpu
from jax.sharding import PartitionSpec as P

FILTER_LOW = [
    0.23037781330885523,
    0.7148465705525415,
    0.6308807679295904,
    -0.02798376941698385,
    -0.18703481171888114,
    0.030841381835986965,
    0.032883011666982945,
    -0.010597401784997278,
]
FILTER_HIGH = [(-1.0) ** offset * FILTER_LOW[7 - offset] for offset in range(8)]
STEP_PRIMAL = 0.5
STEP_DUAL = 1.0
LANES = 128
VMEM_BYTES = 24 * 1024 * 1024
BACK_VMEM_BYTES = 60 * 1024 * 1024
PARTS = 4


def taps(filters, offset):
    table = np.asarray(filters, np.float64)
    valid = (offset >= 0) & (offset < 8)
    return np.where(valid, table[np.clip(offset, 0, 7)], 0.0)


def split_constant(matrix):
    matrix = matrix.astype(np.float32)
    high = matrix.astype(ml_dtypes.bfloat16)
    low = (matrix - high.astype(np.float32)).astype(ml_dtypes.bfloat16)
    return jnp.asarray(np.stack([high, low]))


def split(values):
    high = values.astype(jnp.bfloat16)
    low = (values - high.astype(jnp.float32)).astype(jnp.bfloat16)
    return high, low


def product(a, b):
    return jnp.dot(a, b, preferred_element_type=jnp.float32)


def product_left(matrix, values):
    high, low = split(values)
    return product(matrix[0], high) + product(matrix[0], low) + product(matrix[1], high)


def part_rows(rows):
    half = rows // 2
    a = [row if row < half // 2 else row + half for row in range(half)]
    b = [row + half if row < half // 2 else row for row in range(half)]
    return np.array(a), np.array(b)


def synthesis_rows(channels, rows):
    coef = np.arange(rows // 2)[None, :]
    a, b = part_rows(rows)
    sides = (-3, -2, -1, rows, rows + 1, rows + 2)
    blocks = []
    for filters in (FILTER_LOW, FILTER_HIGH):
        parts = [np.kron(np.eye(channels), taps(filters, p[:, None] - 2 * coef + 3)) for p in (a, b)]
        parts += [np.kron(np.eye(channels), taps(filters, row - 2 * coef + 3)) for row in sides]
        blocks.append(np.concatenate(parts, axis=0))
    return np.concatenate(blocks, axis=1)


def synthesis_columns():
    coef = np.arange(3 * LANES)[:, None] - LANES
    pixel = np.arange(2 * LANES)[None, :]
    return np.concatenate(
        [taps(filters, pixel - 2 * coef + 3) for filters in (FILTER_LOW, FILTER_HIGH)], axis=0
    )


def analysis_rows(channels, rows):
    coef = np.arange(rows // 2)[:, None]
    a, b = part_rows(rows)
    sides = (-3, -2, -1, rows, rows + 1, rows + 2)
    bands = []
    for filters in (FILTER_LOW, FILTER_HIGH):
        parts = [np.kron(np.eye(channels), taps(filters, p[None, :] - 2 * coef + 3)) for p in (a, b)]
        parts += [np.kron(np.eye(channels), taps(filters, row - 2 * coef + 3)) for row in sides]
        bands.append(np.concatenate(parts, axis=1))
    return np.concatenate(bands, axis=0)


def analysis_columns():
    pixel = np.arange(4 * LANES)[:, None] - LANES
    coef = np.arange(LANES)[None, :]
    return np.concatenate(
        [taps(filters, pixel - 2 * coef + 3) for filters in (FILTER_LOW, FILTER_HIGH)], axis=1
    )


def border_rows(channels, rows):
    a, _ = part_rows(rows)
    ends = (0, 1, 2, rows - 3, rows - 2, rows - 1)
    picked = [np.kron(np.eye(channels), a[None, :] == row) for row in ends]
    return np.concatenate(picked, axis=0).astype(ml_dtypes.bfloat16)


def back_kernel(
    vis_ref, tile_ref, kernel_hbm, pattern_hbm, out_hbm,
    kernel_ref, pattern_ref, cells_ref, out_ref, sems, out_sems, *, rows,
):
    count = tile_ref.shape[1]
    step = 512
    steps = count // step
    half = rows // 2
    parts = out_ref.shape[0]
    slots = out_ref.shape[1]

    def copies(index):
        at = pl.ds(index * step, step)
        return (
            pltpu.make_async_copy(pattern_hbm.at[at, :], pattern_ref.at[at, :], sems.at[0, index]),
            pltpu.make_async_copy(kernel_hbm.at[at, :], kernel_ref.at[at, :], sems.at[1, index]),
        )

    def copy_out(part):
        return pltpu.make_async_copy(
            out_ref.at[part], out_hbm.at[pl.ds(part * slots, slots), :], out_sems.at[part]
        )

    for index in range(steps):
        for copy in copies(index):
            copy.start()

    tile = tile_ref[...]
    row = tile >> 2
    within = row & (rows - 1)
    in_b = ((within >> 2) ^ (within >> 3)) & 1
    place = (row - within) + half * in_b + (within & (half - 1))
    iota = lax.broadcasted_iota(jnp.int32, (slots, step), 0)
    values = vis_ref[...].astype(jnp.float32)

    for part in range(parts):
        total = None
        for index in range(steps):
            at = slice(index * step, (index + 1) * step)
            if part == 0:
                for copy in copies(index):
                    copy.wait()
                lane_tile = jnp.transpose(jnp.broadcast_to(tile[:, at] & 3, (LANES, step)))
                kept = jnp.where(pattern_ref[at, :] != 0, lane_tile, 4)
                kernels = kernel_ref[at, :].astype(jnp.float32)
                for column in range(4):
                    cells_ref[at, column * LANES : (column + 1) * LANES] = jnp.where(
                        kept == column, kernels, 0.0
                    ).astype(jnp.bfloat16)
            here = place[:, at] - part * slots == iota
            spread = jnp.where(here, values[:, at], 0.0).astype(jnp.bfloat16)
            term = product(spread, cells_ref[at, :])
            total = term if total is None else total + term
        out_ref[part] = total
        copy_out(part).start()
    for part in range(parts):
        copy_out(part).wait()


def back_project(vis, tile, kernels, pattern, rows, facets, quarter):
    count = tile.shape[1]
    parts = PARTS
    slots = rows * facets // parts
    vmem = pl.BlockSpec(memory_space=pltpu.VMEM)
    hbm = pl.BlockSpec(memory_space=pl.ANY)
    return pl.pallas_call(
        functools.partial(back_kernel, rows=rows),
        in_specs=[vmem, vmem, hbm, hbm],
        out_specs=hbm,
        out_shape=jax.ShapeDtypeStruct((rows * facets, quarter), jnp.float32),
        scratch_shapes=[
            pltpu.VMEM((count, LANES), kernels.dtype),
            pltpu.VMEM((count, LANES), pattern.dtype),
            pltpu.VMEM((count, quarter), jnp.bfloat16),
            pltpu.VMEM((parts, slots, quarter), jnp.float32),
            pltpu.SemaphoreType.DMA((2, count // 512)),
            pltpu.SemaphoreType.DMA((parts,)),
        ],
        compiler_params=pltpu.CompilerParams(vmem_limit_bytes=BACK_VMEM_BYTES),
        cost_estimate=pl.CostEstimate(
            flops=2 * rows * facets * count * quarter, bytes_accessed=6 << 20, transcendentals=0
        ),
        name="back_project",
    )(vis, tile, kernels, pattern)


def pick_part(natural, part):
    half = natural.shape[2]
    first = lax.broadcasted_iota(jnp.int32, natural[:, 0].shape, 1) < half // 2
    one, two = (natural[:, 0], natural[:, 1]) if part == 0 else (natural[:, 1], natural[:, 0])
    return jnp.where(first, one, two).reshape(-1, natural.shape[3])


def synthesis_kernel(dual_ref, primal_ref, rows_ref, columns_ref, a_ref, b_ref, above_ref, below_ref, mid_ref):
    tiles = dual_ref.shape[2] // LANES
    for kind in range(2):
        for at in range(0, tiles, 2):
            lanes = slice(at * LANES, (at + 2) * LANES)
            stacked = jnp.concatenate([dual_ref[kind, :, lanes], dual_ref[kind + 2, :, lanes]], axis=0)
            high, low = split(product_left(rows_ref, stacked))
            mid_ref[kind, 0, :, lanes] = high
            mid_ref[kind, 1, :, lanes] = low
    half = a_ref.shape[0]
    side = above_ref.shape[0]
    for at in range(tiles):
        first, last = max(at - 1, 0), min(at + 2, tiles)
        lanes = slice(first * LANES, last * LANES)
        total = 0.0
        for kind in range(2):
            base = (3 * kind + first - at + 1) * LANES
            part = slice(base, base + (last - first) * LANES)
            total = total + product(mid_ref[kind, 0, :, lanes], columns_ref[0, part, :])
            total = total + product(mid_ref[kind, 1, :, lanes], columns_ref[0, part, :])
            total = total + product(mid_ref[kind, 0, :, lanes], columns_ref[1, part, :])
        pixels = slice(2 * at * LANES, 2 * (at + 1) * LANES)
        primal = primal_ref[:, :, :, pixels]
        a_ref[:, pixels] = pick_part(primal, 0) - STEP_PRIMAL * total[:half]
        b_ref[:, pixels] = pick_part(primal, 1) - STEP_PRIMAL * total[half : 2 * half]
        above_ref[:, pixels] = total[2 * half : 2 * half + side]
        below_ref[:, pixels] = total[2 * half + side :]


def synthesize(dual, primal):
    channels, _, half, columns = primal.shape
    part = jax.ShapeDtypeStruct((channels * half, columns), jnp.float32)
    side = jax.ShapeDtypeStruct((3 * channels, columns), jnp.float32)
    rows = split_constant(synthesis_rows(channels, 2 * half))
    return pl.pallas_call(
        synthesis_kernel,
        out_shape=[part, part, side, side],
        scratch_shapes=[pltpu.VMEM((2, 2, rows.shape[1], columns // 2), jnp.bfloat16)],
        compiler_params=pltpu.CompilerParams(vmem_limit_bytes=VMEM_BYTES),
        cost_estimate=pl.CostEstimate(flops=8 << 30, bytes_accessed=8 << 20, transcendentals=0),
        name="synthesis",
    )(dual, primal, rows, split_constant(synthesis_columns()))


def border_kernel(
    me_ref, base_ref, own_ref, one_ref, two_ref, three_ref, primal_ref, pick_ref,
    image_ref, first_ref, last_ref,
):
    base = base_ref[...]
    for step, back_ref in enumerate((own_ref, one_ref, two_ref, three_ref)):

        @pl.when(pl.program_id(0) == step)
        def _(back_ref=back_ref):
            back = back_ref[...].reshape(base.shape)
            image_ref[...] = jnp.maximum(base - STEP_PRIMAL * back, 0.0)

    high, low = split(2.0 * image_ref[...] - pick_part(primal_ref[...], 0))
    picked = product(pick_ref[...], high) + product(pick_ref[...], low)
    half = picked.shape[0] // 2
    first_ref[...] = picked[:half]
    last_ref[...] = picked[half:]


def sides_kernel(base_ref, above_ref, below_ref, place_ref, out_ref):
    high, low = split(jnp.concatenate([above_ref[...], below_ref[...]], axis=0))
    added = product(place_ref[...], high) + product(place_ref[...], low)
    out_ref[...] = base_ref[...] - STEP_PRIMAL * added


def add_sides(base, above, below):
    pixels, columns = base.shape
    channels = above.shape[0] // 3
    place = border_rows(channels, 2 * pixels // channels).T
    return pl.pallas_call(
        sides_kernel,
        out_shape=jax.ShapeDtypeStruct(base.shape, jnp.float32),
        compiler_params=pltpu.CompilerParams(vmem_limit_bytes=VMEM_BYTES),
        cost_estimate=pl.CostEstimate(flops=1 << 30, bytes_accessed=3 << 20, transcendentals=0),
        name="add_sides",
    )(base, above, below, jnp.asarray(place))


def own_part(parts, part):
    _, channels, _, half, quarter = parts.shape
    return pl.BlockSpec((1, channels, 1, half, quarter), lambda i, me: (me[0], 0, part, 0, 0))


def update_border(me, base, parts, backs, primal):
    pixels, columns = base.shape
    channels, _, half, _ = primal.shape
    groups = parts.shape[0]
    quarter = columns // groups
    pick = border_rows(channels, 2 * half)
    block = pl.BlockSpec((pixels, quarter), lambda i, me: (0, i ^ me[0]))
    side = pl.BlockSpec((3 * channels, quarter), lambda i, me: (0, i ^ me[0]))
    whole = lambda i, me: (0, 0)
    side_shape = jax.ShapeDtypeStruct((3 * channels, columns), jnp.float32)
    return pl.pallas_call(
        border_kernel,
        grid_spec=pltpu.PrefetchScalarGridSpec(
            num_scalar_prefetch=1,
            grid=(groups,),
            in_specs=[block, own_part(parts, 0)]
            + [pl.BlockSpec((pixels, quarter), whole)] * len(backs)
            + [
                pl.BlockSpec((channels, 2, half, quarter), lambda i, me: (0, 0, 0, i ^ me[0])),
                pl.BlockSpec(pick.shape, whole),
            ],
            out_specs=[block, side, side],
        ),
        out_shape=[jax.ShapeDtypeStruct(base.shape, jnp.float32), side_shape, side_shape],
        compiler_params=pltpu.CompilerParams(vmem_limit_bytes=VMEM_BYTES),
        cost_estimate=pl.CostEstimate(flops=4 << 20, bytes_accessed=8 << 20, transcendentals=0),
        name="update_border",
    )(me, base, parts, *backs, primal, jnp.asarray(pick))


def finish_kernel(
    me_ref, image_a_ref, base_b_ref, own_ref, one_ref, two_ref, three_ref, primal_ref, above_ref,
    below_ref, dual_ref, rows_ref, columns_ref, image_ref, update_ref, squares_ref, mid_ref, back_ref,
):
    step = pl.program_id(0)
    channels, _, half, width = image_ref.shape
    edge = LANES
    columns = mid_ref.shape[2] - 2 * edge
    blocks = columns // width

    @pl.when(step == 0)
    def _():
        zeros = jnp.zeros(mid_ref.shape[:2] + (edge,), mid_ref.dtype)
        mid_ref[:, :, :edge] = zeros
        mid_ref[:, :, edge + columns :] = zeros

    for part, part_ref in enumerate((own_ref, one_ref, two_ref, three_ref)):

        @pl.when((step ^ me_ref[0]) == part)
        def _(part_ref=part_ref):
            back_ref[...] = part_ref[...].reshape(back_ref.shape)

    @pl.when(step < blocks)
    def _():
        image_b = jnp.maximum(base_b_ref[...] - STEP_PRIMAL * back_ref[...], 0.0)
        image_a = image_a_ref[...]
        wide_a = image_a.reshape(channels, half, width)
        wide_b = image_b.reshape(channels, half, width)
        first = lax.broadcasted_iota(jnp.int32, wide_a.shape, 1) < half // 2
        image_ref[:, 0] = jnp.where(first, wide_a, wide_b)
        image_ref[:, 1] = jnp.where(first, wide_b, wide_a)
        primal = primal_ref[...]
        stacked = jnp.concatenate(
            [
                2.0 * image_a - pick_part(primal, 0),
                2.0 * image_b - pick_part(primal, 1),
                above_ref[...],
                below_ref[...],
            ],
            axis=0,
        )
        high, low = split(product_left(rows_ref, stacked))
        at = pl.ds(pl.multiple_of(edge + step * width, LANES), width)
        mid_ref[0, :, at] = high
        mid_ref[1, :, at] = low

    rows = mid_ref.shape[1] // 2

    @pl.when(step > 0)
    def _():
        for block in range(width // (2 * LANES)):
            start = pl.multiple_of((step - 1) * width + block * 2 * LANES, LANES)
            high = mid_ref[0, :, pl.ds(start, 4 * LANES)]
            low = mid_ref[1, :, pl.ds(start, 4 * LANES)]
            both = product(high, columns_ref[0]) + product(low, columns_ref[0])
            both = both + product(high, columns_ref[1])
            out = slice(block * LANES, (block + 1) * LANES)
            for band in range(4):
                here = slice(band // 2 * rows, (band // 2 + 1) * rows)
                cols = slice(band % 2 * LANES, (band % 2 + 1) * LANES)
                update = dual_ref[band, :, out] + STEP_DUAL * both[here, cols]
                update_ref[band, :, out] = update
                squares = update * update
                squares_ref[band, :, out] = jnp.sum(squares.reshape(-1, half, LANES), axis=0)


def finish(me, image_a, base_b, parts, core_b, far_b, primal, above, below, dual):
    channels, _, half, columns = primal.shape
    rows = split_constant(analysis_rows(channels, 2 * half))
    taps_across = split_constant(analysis_columns())
    blocks = parts.shape[0]
    width = columns // blocks
    pixels = channels * half
    now = lambda i, me: (0, jnp.minimum(i, blocks - 1))
    now4 = lambda i, me: (0, 0, 0, jnp.minimum(i, blocks - 1))
    before = lambda i, me: (0, 0, jnp.maximum(i - 1, 0))
    whole3 = lambda i, me: (0, 0, 0)
    part = pl.BlockSpec((pixels, width), now)
    side = pl.BlockSpec((3 * channels, width), now)
    return pl.pallas_call(
        finish_kernel,
        grid_spec=pltpu.PrefetchScalarGridSpec(
            num_scalar_prefetch=1,
            grid=(blocks + 1,),
            in_specs=[
                part,
                part,
                own_part(parts, 1),
                pl.BlockSpec((1, pixels, width), whole3),
                pl.BlockSpec((1, pixels, width), whole3),
                pl.BlockSpec((1, pixels, width), lambda i, me: (1, 0, 0)),
                pl.BlockSpec((channels, 2, half, width), now4),
                side,
                side,
                pl.BlockSpec((4, pixels, width // 2), before),
                pl.BlockSpec(rows.shape, whole3),
                pl.BlockSpec(taps_across.shape, whole3),
            ],
            out_specs=[
                pl.BlockSpec((channels, 2, half, width), now4),
                pl.BlockSpec((4, pixels, width // 2), before),
                pl.BlockSpec((4, half, width // 2), before),
            ],
            scratch_shapes=[
                pltpu.VMEM((2, rows.shape[1], columns + 2 * LANES), jnp.bfloat16),
                pltpu.VMEM((pixels, width), jnp.float32),
            ],
        ),
        out_shape=[
            jax.ShapeDtypeStruct(primal.shape, jnp.float32),
            jax.ShapeDtypeStruct(dual.shape, jnp.float32),
            jax.ShapeDtypeStruct((4, half, dual.shape[2]), jnp.float32),
        ],
        compiler_params=pltpu.CompilerParams(vmem_limit_bytes=VMEM_BYTES),
        cost_estimate=pl.CostEstimate(flops=4 << 30, bytes_accessed=12 << 20, transcendentals=0),
        name="finish",
    )(me, image_a, base_b, parts, core_b, far_b, far_b, primal, above, below, dual, rows, taps_across)


def project_kernel(update_ref, weight_ref, one_ref, two_ref, three_ref, four_ref, out_ref):
    total = (one_ref[0] + two_ref[0]) + (three_ref[0] + four_ref[0])
    weight = weight_ref[0]
    factor = weight / jnp.maximum(jnp.sqrt(total), weight)
    count = factor.shape[0]
    for channel in range(update_ref.shape[1] // count):
        rows = slice(channel * count, (channel + 1) * count)
        out_ref[0, rows, :] = update_ref[0, rows, :] * factor


def project(update, weight, sums):
    bands, pixels, columns = update.shape
    wide = pl.BlockSpec((1, pixels, columns), lambda i: (i, 0, 0))
    narrow = pl.BlockSpec((1, weight.shape[1], columns), lambda i: (i, 0, 0))
    return pl.pallas_call(
        project_kernel,
        grid=(bands,),
        in_specs=[wide] + [narrow] * 5,
        out_specs=wide,
        out_shape=jax.ShapeDtypeStruct(update.shape, jnp.float32),
        compiler_params=pltpu.CompilerParams(vmem_limit_bytes=VMEM_BYTES),
        cost_estimate=pl.CostEstimate(flops=4 << 20, bytes_accessed=5 << 20, transcendentals=0),
        name="project",
    )(update, weight, *sums)


def shards(
    primal_image, dual_coef, l21_weight, visibilities, tile_index, kernel_values, kernel_pattern
):
    facets, groups = lax.axis_size("fac"), lax.axis_size("chan")
    channels, rows, columns = primal_image.shape
    quarter = columns // groups
    half = rows // 2
    forward = [(i, i + 1) for i in range(facets - 1)]
    backward = [(b, a) for a, b in forward]
    me = lax.axis_index("chan")
    primal = primal_image.reshape(channels, 2, half, columns)
    dual = dual_coef.reshape(4, channels * half, columns // 2)

    grid = back_project(
        visibilities, tile_index, kernel_values[0], kernel_pattern[0], rows, facets, quarter
    )
    by_facet = lax.all_to_all(
        grid.reshape(facets, rows, quarter), "fac", split_axis=0, concat_axis=0, tiled=True
    )
    dual_here, _ = lax.optimization_barrier((dual, grid))
    base_a, base_b, to_above, to_below = synthesize(dual_here, primal)
    from_above = lax.ppermute(to_below, "fac", forward)
    from_below = lax.ppermute(to_above, "fac", backward)
    by_facet, from_above, from_below = lax.optimization_barrier((by_facet, from_above, from_below))
    base_a = add_sides(base_a, from_above, from_below)

    parts = by_facet.reshape(groups, channels, 2, half, quarter)

    def piece(part, step):
        return lax.dynamic_index_in_dim(parts[:, :, part], me ^ step, 0, False).reshape(-1, quarter)

    def pairs(step):
        return [(i, i ^ step) for i in range(groups)]

    sent_a = [piece(0, step) for step in (1, 2, 3)]
    sent_b = jnp.stack([piece(1, 1), piece(1, 3)])
    kept_b = piece(1, 2)
    sent_a, sent_b, kept_b = lax.optimization_barrier((sent_a, sent_b, kept_b))
    backs_a = [lax.ppermute(sent_a[step - 1], "chan", pairs(step)) for step in (1, 2, 3)]
    core_b = lax.ppermute(sent_b, "chan", pairs(1))
    far_b = lax.ppermute(jnp.stack([kept_b, core_b[1]]), "chan", pairs(2))
    me = me.astype(jnp.int32).reshape(1)
    image_a, first, last = update_border(me, base_a, parts, backs_a, primal)
    above = lax.ppermute(last, "fac", forward)
    below = lax.ppermute(first, "fac", backward)
    image, update, squares = finish(
        me, image_a, base_b, parts, core_b, far_b, primal, above, below, dual
    )
    sums = [squares]
    for step in range(1, groups):
        pairs = [(i, i ^ step) for i in range(groups)]
        sums.append(lax.ppermute(squares, "chan", pairs))
    dual_next = project(update, l21_weight, sums)
    return (image.reshape(primal_image.shape), dual_next.reshape(dual_coef.shape))


def solution(mesh):
    in_specs = (
        P("chan", "fac", None),
        P(None, "chan", "fac", None),
        P(None, "fac", None),
        P("fac", "chan"),
        P("fac", "chan"),
        P("fac", "chan", None),
        P("fac", "chan", None),
    )
    out_specs = (P("chan", "fac", None), P(None, "chan", "fac", None))
    return jax.shard_map(shards, mesh=mesh, in_specs=in_specs, out_specs=out_specs, check_vma=False)
```

time: 164 us -> 136 us (0.83)
  blocking collectives: 63.5 us -> 0 us
  waiting for transfers between devices: 32.4 us -> 60.8 us
  starting transfers between devices: 23.3 us -> 40.6 us
  local copies, waits for them, and re-layouts: 12.8 us -> 6.51 us
  Pallas kernels: 30.3 us -> 26.2 us
    all_to_all x1 -> x0, blocking collectives: 63.5 us -> none  [shards(): lax.all_to_all(gridded.reshape(facets, rows, quarter), 'fac', split_axis=...]
    ppermute x2 -> x7, waiting for transfers between devices: 11.6 us -> 44.8 us  [the longest x1 35.9 us: shards(): from_above = lax.ppermute(to_below, 'fac', forward)]
    all_to_all x1, starting transfers between devices: 3.99 us -> 13.2 us  [shards(): lax.all_to_all(grid.reshape(facets, rows, quarter), 'fac', split_axis=0,...]
    ppermute x2 -> x7, starting transfers between devices: 8.85 us -> 15.2 us  [the longest x1 5.48 us: shards(): from_below = lax.ppermute(to_above, 'fac', backward)]
    all_to_all x1, waiting for transfers between devices: 5.62 us -> 0.01 us  [shards(): lax.all_to_all(grid.reshape(facets, rows, quarter), 'fac', split_axis=0,...]
    pallas_call x4 -> x5, Pallas kernels: 28.4 us -> 24.3 us  [the longest x1 8.97 us: back_project(): pl.pallas_call(functools.partial(back_kernel, rows=rows), in_specs=[vmem,...]
    slice x3 -> x2, local copies, waits for them, and re-layouts: 3.44 us -> 0.22 us  [the longest x1 0.2 us: piece(): parts[:, :, part]]
    unnamed x28 -> x30, local copies, waits for them, and re-layouts: 8.77 us -> 6.16 us
  transfers between devices with their start and end apart: 8 -> 13, of which waited for: 8 -> 8; matrix products, arithmetic and copies ran while one was open for 2% -> 0% of each run, Pallas kernels for 4% -> 6%
where the time goes in v1:
time: 136 us; the launch traced here: 135 us
  waiting for transfers between devices  60.8 us (45%)
  starting transfers between devices  40.6 us (30%)
  Pallas kernels  26.2 us (19%)
  local copies, waits for them, and re-layouts  6.51 us (5%)
    ppermute x1, waiting for transfers between devices, shards(): from_above = lax.ppermute(to_below, 'fac', forward)  35.9 us
    all_to_all x1, starting transfers between devices, shards(): lax.all_to_all(grid.reshape(facets, rows, quarter), 'fac', split_axis=0,...  13.2 us
    pallas_call x1, Pallas kernels, back_project(): pl.pallas_call(functools.partial(back_kernel, rows=rows), in_specs=[vmem,...  8.97 us
    ppermute x3, waiting for transfers between devices, shards(): lax.ppermute(sent_a[step - 1], 'chan', pairs(step))  8.7 us
    ppermute x1, waiting for transfers between devices, shards(): above = lax.ppermute(last, 'fac', forward)  8.01 us
    pallas_call x1, Pallas kernels, finish(): pl.pallas_call(finish_kernel, grid_spec=pltpu.PrefetchScalarGridSpec(num_...  7.19 us
    ppermute x1, starting transfers between devices, shards(): below = lax.ppermute(first, 'fac', backward)  6.93 us
    ppermute x3, waiting for transfers between devices, shards(): sums.append(lax.ppermute(squares, 'chan', pairs))  6.74 us
  transfers between devices with their start and end apart: 13, of which 8 were waited for; matrix products, arithmetic and copies ran while one was open for 0% of the time, Pallas kernels for 6%

profile of v1, /device:TPU:8, one launch (start us, length us, event | category | flops | bytes accessed | tf_op | source)
XLA Modules:
  0.0 135.0 jit_solution(1583929680252239619)
XLA Ops:
  0.6 9.0 %back_project.1 = f32[1024,512]{1,0:T(8,128)} custom-call(bf16[1,4096]{1,0:T(2,128)(2,1)} %vis_ref.1, s32[1,4096]{1,0:T(1,128)} %tile_ref.1, bf16[4096,128]{1,0:T(8,128)(2,1)} %bitcast.34, s32[4096,128]{1,0:T(8,128)} %bitcast.33), custom_call_target="tpu_custom_call" | custom-call | flops 4294967296 | bytes 6291456 | tf_op jit(solution)/shard_map/back_project/pallas_call | solution.py:178
  9.6 0.0 copy-start.6
  9.6 13.2 %all-to-all-start = ((f32[64,16,512]{2,1,0:T(8,128)}), f32[64,16,512]{2,1,0:T(8,128)S(1)}, u32[]{:S(2)}, u32[]{:S(2)}) async-start(f32[64,16,512]{2,1,0:T(8,128)} %bitcast.31), calls=%async_computation | async-start | bytes 4194304 | tf_op jit(solution)/shard_map/all_to_all | solution.py:484
  22.8 0.0 copy-done.6
  22.8 0.0 copy-start
  22.8 1.6 %copy-done = f32[16,16,2048]{2,1,0:T(8,128)S(1)} copy-done((f32[16,16,2048]{2,1,0:T(8,128)S(1)}, f32[16,16,2048]{2,1,0:T(8,128)}, u32[]{:S(2)}) %copy-start) | copy-done | bytes 2097176
  24.4 0.0 copy-start.4
  24.4 1.6 %copy-done.4 = f32[4,16,8,1024]{3,2,1,0:T(8,128)S(1)} copy-done((f32[4,16,8,1024]{3,2,1,0:T(8,128)S(1)}, f32[4,16,8,1024]{3,2,1,0:T(8,128)}, u32[]{:S(2)}) %copy-start.4) | copy-done | bytes 2097176
  26.0 0.0 copy-start.9
  26.0 1.0 copy-done.9
  27.0 6.0 %synthesis.1 = (f32[128,2048]{1,0:T(8,128)S(1)}, f32[128,2048]{1,0:T(8,128)S(1)}, f32[48,2048]{1,0:T(8,128)S(1)}, f32[48,2048]{1,0:T(8,128)}) custom-call(f32[4,128,1024]{2,1,0:T(8,128)S(1)} %bitcast.28, f32[16,2,8,2048]{3,2,1,0:T(8,128)S(1)} %bitcast.25, bf16[2,352,256]{2,1,0:T(8,128)(2,1)S(1)} %copy-done.9, bf16[2,768,256]{2,1,0:T(8,128)(2,1)S(1)} %copy-done.6), custom_call_target="tpu_custom_call" | custom-call | flops 8589934592 | bytes 8388608 | tf_op jit(solution)/shard_map/synthesis/pallas_call | solution.py:240
  33.0 0.0 copy-start.11
  33.0 1.0 copy-done.11
  33.9 0.0 copy-start.13
  33.9 1.0 copy-done.13
  34.9 3.4 %collective-permute-start = (f32[48,2048]{1,0:T(8,128)}, f32[48,2048]{1,0:T(8,128)S(1)}, u32[]{:S(2)}, u32[]{:S(2)}) collective-permute-start(f32[48,2048]{1,0:T(8,128)} %get-tuple-element.23), channel_id=1, source_target_pairs={{0,4},{4,8},{8,12},{12,16},{16,20},{20,24},{24,28},{28,32},{32,36}... | collective-permute-start | bytes 1179656 | tf_op jit(solution)/shard_map/ppermute | solution.py:489
  38.3 5.5 %collective-permute-start.1 = (f32[48,2048]{1,0:T(8,128)S(1)}, f32[48,2048]{1,0:T(8,128)S(1)}, u32[]{:S(2)}, u32[]{:S(2)}) collective-permute-start(f32[48,2048]{1,0:T(8,128)S(1)} %get-tuple-element.24), channel_id=1, source_target_pairs={{4,0},{8,4},{12,8},{16,12},{20,16},{24,20},{28,24},{32,28},{36,32}... | collective-permute-start | bytes 1179656 | tf_op jit(solution)/shard_map/ppermute | solution.py:490
  43.8 35.9 %collective-permute-done.above_ref = f32[48,2048]{1,0:T(8,128)S(1)} collective-permute-done((f32[48,2048]{1,0:T(8,128)}, f32[48,2048]{1,0:T(8,128)S(1)}, u32[]{:S(2)}, u32[]{:S(2)}) %collective-permute-start) | collective-permute-done | bytes 393248 | tf_op jit(solution)/shard_map/ppermute | solution.py:489
  79.7 0.0 collective-permute-done.1.below_ref
  79.7 0.0 all-to-all-done
  79.7 0.2 fusion
  79.9 0.1 dynamic-slice_bitcast_fusion
  80.1 0.0 copy-start.10
  80.1 0.0 copy-start.12
  80.1 0.1 collective-permute-start.5
  80.2 0.5 collective-permute-start.2
  80.7 2.7 %collective-permute-start.3 = (f32[128,512]{1,0:T(8,128)S(1)}, f32[128,512]{1,0:T(8,128)S(1)}, u32[]{:S(2)}, u32[]{:S(2)}) collective-permute-start(f32[128,512]{1,0:T(8,128)S(1)} %get-tuple-element.29), channel_id=1, source_target_pairs={{0,2},{1,3},{2,0},{3,1},{4,6},{5,7},{6,4},{7,5},{8,10},{9,11},{10,... | collective-permute-start | bytes 786440 | tf_op jit(solution)/shard_map/ppermute | solution.py:506
  83.5 0.2 collective-permute-start.4
  83.7 0.0 collective-permute-done.5.one_ref
  83.8 0.0 copy-start.1
  83.8 0.0 copy-start.3
  83.8 2.8 %collective-permute-start.6 = (f32[2,128,512]{2,1,0:T(8,128)S(1)}, f32[2,128,512]{2,1,0:T(8,128)S(1)}, u32[]{:S(2)}, u32[]{:S(2)}) collective-permute-start(f32[2,128,512]{2,1,0:T(8,128)S(1)} %pad_maximum_fusion.1), channel_id=1, source_target_pairs={{0,2},{1,3},{2,0},{3,1},{4,6},{5,7},{6,4},{7,5},{8,10},{9,11},{10,... | collective-permute-start | bytes 1572872 | tf_op jit(solution)/shard_map/ppermute | solution.py:508
  86.6 0.0 copy-done.10
  86.6 0.0 copy-done.12
  86.6 0.4 add_sides.1.base_ref
  87.0 0.0 collective-permute-done.2.one_ref
  87.1 4.3 %collective-permute-done.3.two_ref = f32[128,512]{1,0:T(8,128)S(1)} collective-permute-done((f32[128,512]{1,0:T(8,128)S(1)}, f32[128,512]{1,0:T(8,128)S(1)}, u32[]{:S(2)}, u32[]{:S(2)}) %collective-permute-start.3) | collective-permute-done | bytes 262176 | tf_op jit(solution)/shard_map/ppermute | solution.py:506
  91.4 4.4 %collective-permute-done.4.three_ref = f32[128,512]{1,0:T(8,128)S(1)} collective-permute-done((f32[128,512]{1,0:T(8,128)S(1)}, f32[128,512]{1,0:T(8,128)S(1)}, u32[]{:S(2)}, u32[]{:S(2)}) %collective-permute-start.4) | collective-permute-done | bytes 262176 | tf_op jit(solution)/shard_map/ppermute | solution.py:506
  95.8 0.0 copy-done.1
  95.8 0.0 copy-done.3
  95.8 0.0 copy-start.5
  95.8 0.0 copy-start.7
  95.8 0.0 copy-start.8
  95.8 0.0 copy-start.14
  95.8 1.7 %update_border.1 = (f32[128,2048]{1,0:T(8,128)S(1)}, f32[48,2048]{1,0:T(8,128)S(1)}, f32[48,2048]{1,0:T(8,128)S(1)}) custom-call(s32[1]{0:T(128)} %bitcast.me_ref, f32[128,2048]{1,0:T(8,128)S(1)} %add_sides.1.base_ref, f32[4,16,2,8,512]{4,3,2,1,0:T(8,128)S(1)} %bitcast.23, f32[128,512]{1,0:T(8,128)S(1)} %collective-permute-done.2.one_ref, ...), custom_call_target="tpu_custom_call" | custom-call | flops 4194304 | bytes 8388608 | tf_op jit(solution)/shard_map/update_border/pallas_call | solution.py:303
  97.5 1.9 %collective-permute-start.7 = (f32[48,2048]{1,0:T(8,128)S(1)}, f32[48,2048]{1,0:T(8,128)S(1)}, u32[]{:S(2)}, u32[]{:S(2)}) collective-permute-start(f32[48,2048]{1,0:T(8,128)S(1)} %get-tuple-element.35), channel_id=1, source_target_pairs={{0,4},{4,8},{8,12},{12,16},{16,20},{20,24},{24,28},{28,32},{32,36}... | collective-permute-start | bytes 1179656 | tf_op jit(solution)/shard_map/ppermute | solution.py:511
  99.4 6.9 %collective-permute-start.8 = (f32[48,2048]{1,0:T(8,128)S(1)}, f32[48,2048]{1,0:T(8,128)S(1)}, u32[]{:S(2)}, u32[]{:S(2)}) collective-permute-start(f32[48,2048]{1,0:T(8,128)S(1)} %get-tuple-element.36), channel_id=1, source_target_pairs={{4,0},{8,4},{12,8},{16,12},{20,16},{24,20},{28,24},{32,28},{36,32}... | collective-permute-start | bytes 1179656 | tf_op jit(solution)/shard_map/ppermute | solution.py:512
  106.4 8.0 %collective-permute-done.7.above_ref = f32[48,2048]{1,0:T(8,128)S(1)} collective-permute-done((f32[48,2048]{1,0:T(8,128)S(1)}, f32[48,2048]{1,0:T(8,128)S(1)}, u32[]{:S(2)}, u32[]{:S(2)}) %collective-permute-start.7) | collective-permute-done | bytes 393248 | tf_op jit(solution)/shard_map/ppermute | solution.py:511
  114.4 1.3 collective-permute-done.8.below_ref
  115.7 0.1 collective-permute-done.6.two_ref.three_ref
  115.8 0.0 copy-done.5
  115.8 0.0 copy-done.7
  115.8 0.0 copy-done.8
  115.8 0.0 copy-done.14
  115.9 0.0 copy-start.2
  115.9 7.2 %finish.1 = (f32[16,2,8,2048]{3,2,1,0:T(8,128)}, f32[4,128,1024]{2,1,0:T(8,128)S(1)}, f32[4,8,1024]{2,1,0:T(8,128)S(1)}) custom-call(s32[1]{0:T(128)} %bitcast.me_ref, f32[128,2048]{1,0:T(8,128)S(1)} %get-tuple-element.31.image_a_ref, f32[128,2048]{1,0:T(8,128)S(1)} %copy-done.14, f32[4,16,2,8,512]{4,3,2,1,0:T(8,128)S(1)} %bitcast.24, ...), custom_call_target="tpu_custom_call" | custom-call | flops 4294967296 | bytes 12582912 | tf_op jit(solution)/shard_map/finish/pallas_call | solution.py:402
  123.1 2.1 %collective-permute-start.11 = (f32[4,8,1024]{2,1,0:T(8,128)S(1)}, f32[4,8,1024]{2,1,0:T(8,128)S(1)}, u32[]{:S(2)}, u32[]{:S(2)}) collective-permute-start(f32[4,8,1024]{2,1,0:T(8,128)S(1)} %get-tuple-element.39.one_ref), channel_id=1, source_target_pairs={{0,3},{1,2},{2,1},{3,0},{4,7},{5,6},{6,5},{7,4},{8,11},{9,10},{10,... | collective-permute-start | bytes 393224 | tf_op jit(solution)/shard_map/ppermute | solution.py:519
  125.1 0.9 collective-permute-start.10
  126.0 0.4 collective-permute-start.9
  126.4 3.9 %collective-permute-done.11.four_ref = f32[4,8,1024]{2,1,0:T(8,128)S(1)} collective-permute-done((f32[4,8,1024]{2,1,0:T(8,128)S(1)}, f32[4,8,1024]{2,1,0:T(8,128)S(1)}, u32[]{:S(2)}, u32[]{:S(2)}) %collective-permute-start.11) | collective-permute-done | bytes 131104 | tf_op jit(solution)/shard_map/ppermute | solution.py:519
  130.4 2.8 %collective-permute-done.10.three_ref = f32[4,8,1024]{2,1,0:T(8,128)S(1)} collective-permute-done((f32[4,8,1024]{2,1,0:T(8,128)S(1)}, f32[4,8,1024]{2,1,0:T(8,128)S(1)}, u32[]{:S(2)}, u32[]{:S(2)}) %collective-permute-start.10) | collective-permute-done | bytes 131104 | tf_op jit(solution)/shard_map/ppermute | solution.py:519
  133.2 0.0 collective-permute-done.9.two_ref
  133.2 0.0 copy-done.2
  133.2 1.9 %project.1 = f32[4,128,1024]{2,1,0:T(8,128)} custom-call(f32[4,128,1024]{2,1,0:T(8,128)S(1)} %get-tuple-element.38.update_ref, f32[4,8,1024]{2,1,0:T(8,128)S(1)} %copy-done.2, f32[4,8,1024]{2,1,0:T(8,128)S(1)} %get-tuple-element.39.one_ref, f32[4,8,1024]{2,1,0:T(8,128)S(1)} %collective-permute-done.9.two_ref, ...), custom_call_target="tpu_custom_call" | custom-call | flops 4194304 | bytes 5242880 | tf_op jit(solution)/shard_map/project/pallas_call | solution.py:456
  (3 shorter events, 0.1 us)
Async XLA Ops:
  9.6 13.2 %copy-start.6 = (bf16[2,768,256]{2,1,0:T(8,128)(2,1)S(1)}, bf16[2,768,256]{2,1,0:T(8,128)(2,1)}, u32[]{:S(2)}) copy-start(bf16[2,768,256]{2,1,0:T(8,128)(2,1)} %constant.45.clone.columns_ref) | copy-start | bytes 2359300
  9.6 70.1 %all-to-all-start = ((f32[64,16,512]{2,1,0:T(8,128)}), f32[64,16,512]{2,1,0:T(8,128)S(1)}, u32[]{:S(2)}, u32[]{:S(2)}) async-start(f32[64,16,512]{2,1,0:T(8,128)} %bitcast.31), calls=%async_computation | async-start | bytes 4194304 | tf_op jit(solution)/shard_map/all_to_all | solution.py:484
  22.8 1.6 %copy-start = (f32[16,16,2048]{2,1,0:T(8,128)S(1)}, f32[16,16,2048]{2,1,0:T(8,128)}, u32[]{:S(2)}) copy-start(f32[16,16,2048]{2,1,0:T(8,128)} %param.13) | copy-start | bytes 6291460
  24.4 1.6 %copy-start.4 = (f32[4,16,8,1024]{3,2,1,0:T(8,128)S(1)}, f32[4,16,8,1024]{3,2,1,0:T(8,128)}, u32[]{:S(2)}) copy-start(f32[4,16,8,1024]{3,2,1,0:T(8,128)} %param.14) | copy-start | bytes 6291460
  26.0 1.0 copy-start.9
  33.0 1.0 copy-start.11
  33.9 1.0 copy-start.13
  34.9 44.8 %collective-permute-start = (f32[48,2048]{1,0:T(8,128)}, f32[48,2048]{1,0:T(8,128)S(1)}, u32[]{:S(2)}, u32[]{:S(2)}) collective-permute-start(f32[48,2048]{1,0:T(8,128)} %get-tuple-element.23), channel_id=1, source_target_pairs={{0,4},{4,8},{8,12},{12,16},{16,20},{20,24},{24,28},{28,32},{32,36}... | collective-permute-start | bytes 1179656 | tf_op jit(solution)/shard_map/ppermute | solution.py:489
  38.3 41.4 %collective-permute-start.1 = (f32[48,2048]{1,0:T(8,128)S(1)}, f32[48,2048]{1,0:T(8,128)S(1)}, u32[]{:S(2)}, u32[]{:S(2)}) collective-permute-start(f32[48,2048]{1,0:T(8,128)S(1)} %get-tuple-element.24), channel_id=1, source_target_pairs={{4,0},{8,4},{12,8},{16,12},{20,16},{24,20},{28,24},{32,28},{36,32}... | collective-permute-start | bytes 1179656 | tf_op jit(solution)/shard_map/ppermute | solution.py:490
  80.1 6.5 %copy-start.10 = (bf16[128,96]{1,0:T(8,128)(2,1)S(1)}, bf16[128,96]{1,0:T(8,128)(2,1)}, u32[]{:S(2)}) copy-start(bf16[128,96]{1,0:T(8,128)(2,1)} %constant.46.clone.place_ref) | copy-start | bytes 73732
  80.1 6.5 %copy-start.12 = (f32[128,2048]{1,0:T(8,128)S(1)}, f32[128,2048]{1,0:T(8,128)}, u32[]{:S(2)}) copy-start(f32[128,2048]{1,0:T(8,128)} %copy-done.11) | copy-start | bytes 3145732
  80.1 3.6 %collective-permute-start.5 = (f32[2,128,512]{2,1,0:T(8,128)S(1)}, f32[2,128,512]{2,1,0:T(8,128)S(1)}, u32[]{:S(2)}, u32[]{:S(2)}) collective-permute-start(f32[2,128,512]{2,1,0:T(8,128)S(1)} %pad_maximum_fusion), channel_id=1, source_target_pairs={{0,1},{1,0},{2,3},{3,2},{4,5},{5,4},{6,7},{7,6},{8,9},{9,8},{10,11... | collective-permute-start | bytes 1572872 | tf_op jit(solution)/shard_map/ppermute | solution.py:507
  80.2 6.8 %collective-permute-start.2 = (f32[128,512]{1,0:T(8,128)S(1)}, f32[128,512]{1,0:T(8,128)S(1)}, u32[]{:S(2)}, u32[]{:S(2)}) collective-permute-start(f32[128,512]{1,0:T(8,128)S(1)} %get-tuple-element.28), channel_id=1, source_target_pairs={{0,1},{1,0},{2,3},{3,2},{4,5},{5,4},{6,7},{7,6},{8,9},{9,8},{10,11... | collective-permute-start | bytes 786440 | tf_op jit(solution)/shard_map/ppermute | solution.py:506
  80.7 10.7 %collective-permute-start.3 = (f32[128,512]{1,0:T(8,128)S(1)}, f32[128,512]{1,0:T(8,128)S(1)}, u32[]{:S(2)}, u32[]{:S(2)}) collective-permute-start(f32[128,512]{1,0:T(8,128)S(1)} %get-tuple-element.29), channel_id=1, source_target_pairs={{0,2},{1,3},{2,0},{3,1},{4,6},{5,7},{6,4},{7,5},{8,10},{9,11},{10,... | collective-permute-start | bytes 786440 | tf_op jit(solution)/shard_map/ppermute | solution.py:506
  83.5 12.3 %collective-permute-start.4 = (f32[128,512]{1,0:T(8,128)S(1)}, f32[128,512]{1,0:T(8,128)S(1)}, u32[]{:S(2)}, u32[]{:S(2)}) collective-permute-start(f32[128,512]{1,0:T(8,128)S(1)} %get-tuple-element.30), channel_id=1, source_target_pairs={{0,3},{1,2},{2,1},{3,0},{4,7},{5,6},{6,5},{7,4},{8,11},{9,10},{10,... | collective-permute-start | bytes 786440 | tf_op jit(solution)/shard_map/ppermute | solution.py:506
  83.8 12.0 %copy-start.1 = (f32[16,16,2048]{2,1,0:T(8,128)S(1)}, f32[16,16,2048]{2,1,0:T(8,128)}, u32[]{:S(2)}) copy-start(f32[16,16,2048]{2,1,0:T(8,128)} %param.13) | copy-start | bytes 6291460
  83.8 12.0 %copy-start.3 = (bf16[96,128]{1,0:T(8,128)(2,1)S(1)}, bf16[96,128]{1,0:T(8,128)(2,1)}, u32[]{:S(2)}) copy-start(bf16[96,128]{1,0:T(8,128)(2,1)} %constant.47.clone.pick_ref) | copy-start | bytes 73732
  83.8 32.0 %collective-permute-start.6 = (f32[2,128,512]{2,1,0:T(8,128)S(1)}, f32[2,128,512]{2,1,0:T(8,128)S(1)}, u32[]{:S(2)}, u32[]{:S(2)}) collective-permute-start(f32[2,128,512]{2,1,0:T(8,128)S(1)} %pad_maximum_fusion.1), channel_id=1, source_target_pairs={{0,2},{1,3},{2,0},{3,1},{4,6},{5,7},{6,4},{7,5},{8,10},{9,11},{10,... | collective-permute-start | bytes 1572872 | tf_op jit(solution)/shard_map/ppermute | solution.py:508
  95.8 20.1 %copy-start.5 = (f32[4,16,8,1024]{3,2,1,0:T(8,128)S(1)}, f32[4,16,8,1024]{3,2,1,0:T(8,128)}, u32[]{:S(2)}) copy-start(f32[4,16,8,1024]{3,2,1,0:T(8,128)} %param.14) | copy-start | bytes 6291460
  95.8 20.1 %copy-start.7 = (bf16[2,512,256]{2,1,0:T(8,128)(2,1)S(1)}, bf16[2,512,256]{2,1,0:T(8,128)(2,1)}, u32[]{:S(2)}) copy-start(bf16[2,512,256]{2,1,0:T(8,128)(2,1)} %constant.49.clone.columns_ref) | copy-start | bytes 1572868
  95.8 20.1 %copy-start.8 = (bf16[2,256,352]{2,1,0:T(8,128)(2,1)S(1)}, bf16[2,256,352]{2,1,0:T(8,128)(2,1)}, u32[]{:S(2)}) copy-start(bf16[2,256,352]{2,1,0:T(8,128)(2,1)} %constant.48.clone.rows_ref) | copy-start | bytes 1081348
  95.8 20.1 %copy-start.14 = (f32[128,2048]{1,0:T(8,128)S(1)}, f32[128,2048]{1,0:T(8,128)}, u32[]{:S(2)}) copy-start(f32[128,2048]{1,0:T(8,128)} %copy-done.13) | copy-start | bytes 3145732
  97.5 16.9 %collective-permute-start.7 = (f32[48,2048]{1,0:T(8,128)S(1)}, f32[48,2048]{1,0:T(8,128)S(1)}, u32[]{:S(2)}, u32[]{:S(2)}) collective-permute-start(f32[48,2048]{1,0:T(8,128)S(1)} %get-tuple-element.35), channel_id=1, source_target_pairs={{0,4},{4,8},{8,12},{12,16},{16,20},{20,24},{24,28},{28,32},{32,36}... | collective-permute-start | bytes 1179656 | tf_op jit(solution)/shard_map/ppermute | solution.py:511
  99.4 16.3 %collective-permute-start.8 = (f32[48,2048]{1,0:T(8,128)S(1)}, f32[48,2048]{1,0:T(8,128)S(1)}, u32[]{:S(2)}, u32[]{:S(2)}) collective-permute-start(f32[48,2048]{1,0:T(8,128)S(1)} %get-tuple-element.36), channel_id=1, source_target_pairs={{4,0},{8,4},{12,8},{16,12},{20,16},{24,20},{28,24},{32,28},{36,32}... | collective-permute-start | bytes 1179656 | tf_op jit(solution)/shard_map/ppermute | solution.py:512
  115.9 17.3 %copy-start.2 = (f32[4,8,1024]{2,1,0:T(8,128)S(1)}, f32[4,8,1024]{2,1,0:T(8,128)}, u32[]{:S(2)}) copy-start(f32[4,8,1024]{2,1,0:T(8,128)} %weight_ref.1) | copy-start | bytes 393220
  123.1 7.3 %collective-permute-start.11 = (f32[4,8,1024]{2,1,0:T(8,128)S(1)}, f32[4,8,1024]{2,1,0:T(8,128)S(1)}, u32[]{:S(2)}, u32[]{:S(2)}) collective-permute-start(f32[4,8,1024]{2,1,0:T(8,128)S(1)} %get-tuple-element.39.one_ref), channel_id=1, source_target_pairs={{0,3},{1,2},{2,1},{3,0},{4,7},{5,6},{6,5},{7,4},{8,11},{9,10},{10,... | collective-permute-start | bytes 393224 | tf_op jit(solution)/shard_map/ppermute | solution.py:519
  125.1 8.0 %collective-permute-start.10 = (f32[4,8,1024]{2,1,0:T(8,128)S(1)}, f32[4,8,1024]{2,1,0:T(8,128)S(1)}, u32[]{:S(2)}, u32[]{:S(2)}) collective-permute-start(f32[4,8,1024]{2,1,0:T(8,128)S(1)} %get-tuple-element.39.one_ref), channel_id=1, source_target_pairs={{0,2},{1,3},{2,0},{3,1},{4,6},{5,7},{6,4},{7,5},{8,10},{9,11},{10,... | collective-permute-start | bytes 393224 | tf_op jit(solution)/shard_map/ppermute | solution.py:519
  126.0 7.2 %collective-permute-start.9 = (f32[4,8,1024]{2,1,0:T(8,128)S(1)}, f32[4,8,1024]{2,1,0:T(8,128)S(1)}, u32[]{:S(2)}, u32[]{:S(2)}) collective-permute-start(f32[4,8,1024]{2,1,0:T(8,128)S(1)} %get-tuple-element.39.one_ref), channel_id=1, source_target_pairs={{0,1},{1,0},{2,3},{3,2},{4,5},{5,4},{6,7},{7,6},{8,9},{9,8},{10,11... | collective-permute-start | bytes 393224 | tf_op jit(solution)/shard_map/ppermute | solution.py:519

commit v2 on v1

--- a/solution.py
+++ b/solution.py
@@ -26,6 +26,7 @@
 VMEM_BYTES = 24 * 1024 * 1024
 BACK_VMEM_BYTES = 60 * 1024 * 1024
 PARTS = 4
+RING = 8
 
 
 def taps(filters, offset):
@@ -115,7 +116,7 @@
     kernel_ref, pattern_ref, cells_ref, out_ref, sems, out_sems, *, rows,
 ):
     count = tile_ref.shape[1]
-    step = 512
+    step = 1024
     steps = count // step
     half = rows // 2
     parts = out_ref.shape[0]
@@ -142,8 +143,9 @@
     within = row & (rows - 1)
     in_b = ((within >> 2) ^ (within >> 3)) & 1
     place = (row - within) + half * in_b + (within & (half - 1))
-    iota = lax.broadcasted_iota(jnp.int32, (slots, step), 0)
-    values = vis_ref[...].astype(jnp.float32)
+    iota = lax.broadcasted_iota(jnp.int32, (slots, step), 0).astype(jnp.float32).astype(jnp.bfloat16)
+    values = vis_ref[...]
+    zero = jnp.zeros((), jnp.bfloat16)
 
     for part in range(parts):
         total = None
@@ -154,13 +156,16 @@
                     copy.wait()
                 lane_tile = jnp.transpose(jnp.broadcast_to(tile[:, at] & 3, (LANES, step)))
                 kept = jnp.where(pattern_ref[at, :] != 0, lane_tile, 4)
-                kernels = kernel_ref[at, :].astype(jnp.float32)
+                kept = kept.astype(jnp.float32).astype(jnp.bfloat16)
+                kernels = kernel_ref[at, :]
                 for column in range(4):
                     cells_ref[at, column * LANES : (column + 1) * LANES] = jnp.where(
-                        kept == column, kernels, 0.0
-                    ).astype(jnp.bfloat16)
-            here = place[:, at] - part * slots == iota
-            spread = jnp.where(here, values[:, at], 0.0).astype(jnp.bfloat16)
+                        kept == column, kernels, zero
+                    )
+            local = place[:, at] - part * slots
+            local = jnp.where((local >= 0) & (local < slots), local, -1)
+            local = local.astype(jnp.float32).astype(jnp.bfloat16)
+            spread = jnp.where(local == iota, values[:, at], zero)
             term = product(spread, cells_ref[at, :])
             total = term if total is None else total + term
         out_ref[part] = total
@@ -185,7 +190,7 @@
             pltpu.VMEM((count, LANES), pattern.dtype),
             pltpu.VMEM((count, quarter), jnp.bfloat16),
             pltpu.VMEM((parts, slots, quarter), jnp.float32),
-            pltpu.SemaphoreType.DMA((2, count // 512)),
+            pltpu.SemaphoreType.DMA((2, count // 1024)),
             pltpu.SemaphoreType.DMA((parts,)),
         ],
         compiler_params=pltpu.CompilerParams(vmem_limit_bytes=BACK_VMEM_BYTES),
@@ -247,82 +252,106 @@
     )(dual, primal, rows, split_constant(synthesis_columns()))
 
 
-def border_kernel(
-    me_ref, base_ref, own_ref, one_ref, two_ref, three_ref, primal_ref, pick_ref,
-    image_ref, first_ref, last_ref,
-):
-    base = base_ref[...]
+def own_part(parts, part):
+    _, channels, _, half, quarter = parts.shape
+    return pl.BlockSpec((1, channels, 1, half, quarter), lambda i, me: (me[0], 0, part, 0, 0))
+
+
+def sides_kernel(base_ref, above_ref, below_ref, place_ref, out_ref):
+    high, low = split(jnp.concatenate([above_ref[...], below_ref[...]], axis=0))
+    added = product(place_ref[...], high) + product(place_ref[...], low)
+    out_ref[...] = base_ref[...] - STEP_PRIMAL * added
+
+
+def add_sides(base, above, below):
+    pixels, columns = base.shape
+    channels = above.shape[0] // 3
+    place = border_rows(channels, 2 * pixels // channels).T
+    return pl.pallas_call(
+        sides_kernel,
+        out_shape=jax.ShapeDtypeStruct(base.shape, jnp.float32),
+        compiler_params=pltpu.CompilerParams(vmem_limit_bytes=VMEM_BYTES),
+        cost_estimate=pl.CostEstimate(flops=40 << 30, bytes_accessed=3 << 20, transcendentals=0),
+        name="add_sides",
+    )(base, above, below, jnp.asarray(place))
+
+
+def border_sum_kernel(me_ref, base_ref, own_ref, one_ref, two_ref, three_ref, out_ref):
     for step, back_ref in enumerate((own_ref, one_ref, two_ref, three_ref)):
 
         @pl.when(pl.program_id(0) == step)
         def _(back_ref=back_ref):
-            back = back_ref[...].reshape(base.shape)
-            image_ref[...] = jnp.maximum(base - STEP_PRIMAL * back, 0.0)
-
-    high, low = split(2.0 * image_ref[...] - pick_part(primal_ref[...], 0))
+            out_ref[...] = base_ref[...] - STEP_PRIMAL * back_ref[...].reshape(base_ref.shape)
+
+
+def border_sum(me, base, parts, backs):
+    pixels, columns = base.shape
+    groups = parts.shape[0]
+    quarter = columns // groups
+    block = pl.BlockSpec((pixels, quarter), lambda i, me: (0, i ^ me[0]))
+    whole = lambda i, me: (0, 0)
+    return pl.pallas_call(
+        border_sum_kernel,
+        grid_spec=pltpu.PrefetchScalarGridSpec(
+            num_scalar_prefetch=1,
+            grid=(groups,),
+            in_specs=[block, own_part(parts, 0)]
+            + [pl.BlockSpec((pixels, quarter), whole)] * len(backs),
+            out_specs=block,
+        ),
+        out_shape=jax.ShapeDtypeStruct(base.shape, jnp.float32),
+        compiler_params=pltpu.CompilerParams(vmem_limit_bytes=VMEM_BYTES),
+        cost_estimate=pl.CostEstimate(flops=20 << 30, bytes_accessed=3 << 20, transcendentals=0),
+        name="border_sum",
+    )(me, base, parts, *backs)
+
+
+def border_kernel(
+    base_ref, above_ref, below_ref, primal_ref, pick_ref, place_ref, image_ref, first_ref, last_ref
+):
+    high, low = split(jnp.concatenate([above_ref[...], below_ref[...]], axis=0))
+    added = product(place_ref[...], high) + product(place_ref[...], low)
+    image = jnp.maximum(base_ref[...] - STEP_PRIMAL * added, 0.0)
+    image_ref[...] = image
+    high, low = split(2.0 * image - pick_part(primal_ref[...], 0))
     picked = product(pick_ref[...], high) + product(pick_ref[...], low)
     half = picked.shape[0] // 2
     first_ref[...] = picked[:half]
     last_ref[...] = picked[half:]
 
 
-def sides_kernel(base_ref, above_ref, below_ref, place_ref, out_ref):
-    high, low = split(jnp.concatenate([above_ref[...], below_ref[...]], axis=0))
-    added = product(place_ref[...], high) + product(place_ref[...], low)
-    out_ref[...] = base_ref[...] - STEP_PRIMAL * added
-
-
-def add_sides(base, above, below):
-    pixels, columns = base.shape
-    channels = above.shape[0] // 3
-    place = border_rows(channels, 2 * pixels // channels).T
-    return pl.pallas_call(
-        sides_kernel,
-        out_shape=jax.ShapeDtypeStruct(base.shape, jnp.float32),
-        compiler_params=pltpu.CompilerParams(vmem_limit_bytes=VMEM_BYTES),
-        cost_estimate=pl.CostEstimate(flops=1 << 30, bytes_accessed=3 << 20, transcendentals=0),
-        name="add_sides",
-    )(base, above, below, jnp.asarray(place))
-
-
-def own_part(parts, part):
-    _, channels, _, half, quarter = parts.shape
-    return pl.BlockSpec((1, channels, 1, half, quarter), lambda i, me: (me[0], 0, part, 0, 0))
-
-
-def update_border(me, base, parts, backs, primal):
+def update_border(base, sides, primal):
     pixels, columns = base.shape
     channels, _, half, _ = primal.shape
-    groups = parts.shape[0]
-    quarter = columns // groups
+    blocks = 4
+    width = columns // blocks
     pick = border_rows(channels, 2 * half)
-    block = pl.BlockSpec((pixels, quarter), lambda i, me: (0, i ^ me[0]))
-    side = pl.BlockSpec((3 * channels, quarter), lambda i, me: (0, i ^ me[0]))
-    whole = lambda i, me: (0, 0)
+    block = pl.BlockSpec((pixels, width), lambda i: (0, i))
+    side = pl.BlockSpec((3 * channels, width), lambda i: (0, i))
+    whole = lambda i: (0, 0)
     side_shape = jax.ShapeDtypeStruct((3 * channels, columns), jnp.float32)
     return pl.pallas_call(
         border_kernel,
-        grid_spec=pltpu.PrefetchScalarGridSpec(
-            num_scalar_prefetch=1,
-            grid=(groups,),
-            in_specs=[block, own_part(parts, 0)]
-            + [pl.BlockSpec((pixels, quarter), whole)] * len(backs)
-            + [
-                pl.BlockSpec((channels, 2, half, quarter), lambda i, me: (0, 0, 0, i ^ me[0])),
-                pl.BlockSpec(pick.shape, whole),
-            ],
-            out_specs=[block, side, side],
-        ),
+        grid=(blocks,),
+        in_specs=[
+            block,
+            side,
+            side,
+            pl.BlockSpec((channels, 2, half, width), lambda i: (0, 0, 0, i)),
+            pl.BlockSpec(pick.shape, whole),
+            pl.BlockSpec(pick.shape[::-1], whole),
+        ],
+        out_specs=[block, side, side],
         out_shape=[jax.ShapeDtypeStruct(base.shape, jnp.float32), side_shape, side_shape],
         compiler_params=pltpu.CompilerParams(vmem_limit_bytes=VMEM_BYTES),
-        cost_estimate=pl.CostEstimate(flops=4 << 20, bytes_accessed=8 << 20, transcendentals=0),
+        cost_estimate=pl.CostEstimate(flops=4 << 20, bytes_accessed=4 << 20, transcendentals=0),
         name="update_border",
-    )(me, base, parts, *backs, primal, jnp.asarray(pick))
+    )(base, *sides, primal, jnp.asarray(pick), jnp.asarray(pick.T))
 
 
 def finish_kernel(
-    me_ref, image_a_ref, base_b_ref, own_ref, one_ref, two_ref, three_ref, primal_ref, above_ref,
-    below_ref, dual_ref, rows_ref, columns_ref, image_ref, update_ref, squares_ref, mid_ref, back_ref,
+    me_ref, image_a_ref, base_b_ref, own_ref, one_ref, two_ref, three_ref, primal_ref,
+    dual_ref, rows_ref, columns_ref, image_ref, update_ref, mid_ref, back_ref,
 ):
     step = pl.program_id(0)
     channels, _, half, width = image_ref.shape
@@ -356,8 +385,6 @@
             [
                 2.0 * image_a - pick_part(primal, 0),
                 2.0 * image_b - pick_part(primal, 1),
-                above_ref[...],
-                below_ref[...],
             ],
             axis=0,
         )
@@ -380,15 +407,12 @@
             for band in range(4):
                 here = slice(band // 2 * rows, (band // 2 + 1) * rows)
                 cols = slice(band % 2 * LANES, (band % 2 + 1) * LANES)
-                update = dual_ref[band, :, out] + STEP_DUAL * both[here, cols]
-                update_ref[band, :, out] = update
-                squares = update * update
-                squares_ref[band, :, out] = jnp.sum(squares.reshape(-1, half, LANES), axis=0)
-
-
-def finish(me, image_a, base_b, parts, core_b, far_b, primal, above, below, dual):
+                update_ref[band, :, out] = dual_ref[band, :, out] + STEP_DUAL * both[here, cols]
+
+
+def finish(me, image_a, base_b, parts, core_b, far_b, primal, dual):
     channels, _, half, columns = primal.shape
-    rows = split_constant(analysis_rows(channels, 2 * half))
+    rows = split_constant(analysis_rows(channels, 2 * half)[:, : 2 * channels * half])
     taps_across = split_constant(analysis_columns())
     blocks = parts.shape[0]
     width = columns // blocks
@@ -398,7 +422,6 @@
     before = lambda i, me: (0, 0, jnp.maximum(i - 1, 0))
     whole3 = lambda i, me: (0, 0, 0)
     part = pl.BlockSpec((pixels, width), now)
-    side = pl.BlockSpec((3 * channels, width), now)
     return pl.pallas_call(
         finish_kernel,
         grid_spec=pltpu.PrefetchScalarGridSpec(
@@ -412,8 +435,6 @@
                 pl.BlockSpec((1, pixels, width), whole3),
                 pl.BlockSpec((1, pixels, width), lambda i, me: (1, 0, 0)),
                 pl.BlockSpec((channels, 2, half, width), now4),
-                side,
-                side,
                 pl.BlockSpec((4, pixels, width // 2), before),
                 pl.BlockSpec(rows.shape, whole3),
                 pl.BlockSpec(taps_across.shape, whole3),
@@ -421,7 +442,6 @@
             out_specs=[
                 pl.BlockSpec((channels, 2, half, width), now4),
                 pl.BlockSpec((4, pixels, width // 2), before),
-                pl.BlockSpec((4, half, width // 2), before),
             ],
             scratch_shapes=[
                 pltpu.VMEM((2, rows.shape[1], columns + 2 * LANES), jnp.bfloat16),
@@ -431,16 +451,82 @@
         out_shape=[
             jax.ShapeDtypeStruct(primal.shape, jnp.float32),
             jax.ShapeDtypeStruct(dual.shape, jnp.float32),
-            jax.ShapeDtypeStruct((4, half, dual.shape[2]), jnp.float32),
         ],
         compiler_params=pltpu.CompilerParams(vmem_limit_bytes=VMEM_BYTES),
         cost_estimate=pl.CostEstimate(flops=4 << 30, bytes_accessed=12 << 20, transcendentals=0),
         name="finish",
-    )(me, image_a, base_b, parts, core_b, far_b, far_b, primal, above, below, dual, rows, taps_across)
-
-
-def project_kernel(update_ref, weight_ref, one_ref, two_ref, three_ref, four_ref, out_ref):
-    total = (one_ref[0] + two_ref[0]) + (three_ref[0] + four_ref[0])
+    )(me, image_a, base_b, parts, core_b, far_b, far_b, primal, dual, rows, taps_across)
+
+
+def halo_kernel(
+    main_ref, above_ref, below_ref, rows_ref, columns_ref, update_ref, squares_ref, mid_ref
+):
+    step = pl.program_id(0)
+    edge = LANES
+    columns = above_ref.shape[1]
+    _, _, width = update_ref.shape
+    half = squares_ref.shape[1]
+    count = mid_ref.shape[0] // 2
+
+    @pl.when(step == 0)
+    def _():
+        zeros = jnp.zeros((2 * count, edge), mid_ref.dtype)
+        mid_ref[:, :edge] = zeros
+        mid_ref[:, edge + columns :] = zeros
+        high, low = split(jnp.concatenate([above_ref[...], below_ref[...]], axis=0))
+        mid_ref[:count, edge : edge + columns] = high
+        mid_ref[count:, edge : edge + columns] = low
+
+    rows = rows_ref.shape[1] // 2
+    for block in range(width // LANES):
+        start = pl.multiple_of(2 * (step * width + block * LANES), LANES)
+        window = mid_ref[:, pl.ds(start, 4 * LANES)]
+        once = product(window, columns_ref[0])
+        across = once[:count] + once[count:] + product(window[:count], columns_ref[1])
+        both = product_left(rows_ref, across)
+        out = slice(block * LANES, (block + 1) * LANES)
+        for band in range(4):
+            here = slice(band // 2 * rows, (band // 2 + 1) * rows)
+            cols = slice(band % 2 * LANES, (band % 2 + 1) * LANES)
+            update = main_ref[band, :, out] + STEP_DUAL * both[here, cols]
+            update_ref[band, :, out] = update
+            squares = update * update
+            squares_ref[band, :, out] = jnp.sum(squares.reshape(-1, half, LANES), axis=0)
+
+
+def add_halo(main, above, below, half):
+    _, pixels, columns = main.shape
+    channels = pixels // half
+    rows = split_constant(analysis_rows(channels, 2 * half)[:, 2 * pixels :])
+    taps_across = split_constant(analysis_columns())
+    blocks = 4
+    wide = pl.BlockSpec((4, pixels, columns // blocks), lambda i: (0, 0, i))
+    whole = lambda i: (0, 0)
+    whole3 = lambda i: (0, 0, 0)
+    return pl.pallas_call(
+        halo_kernel,
+        grid=(blocks,),
+        in_specs=[
+            wide,
+            pl.BlockSpec(above.shape, whole),
+            pl.BlockSpec(below.shape, whole),
+            pl.BlockSpec(rows.shape, whole3),
+            pl.BlockSpec(taps_across.shape, whole3),
+        ],
+        out_specs=[wide, pl.BlockSpec((4, half, columns // blocks), lambda i: (0, 0, i))],
+        out_shape=[
+            jax.ShapeDtypeStruct(main.shape, jnp.float32),
+            jax.ShapeDtypeStruct((4, half, columns), jnp.float32),
+        ],
+        scratch_shapes=[pltpu.VMEM((4 * above.shape[0], above.shape[1] + 2 * LANES), jnp.bfloat16)],
+        compiler_params=pltpu.CompilerParams(vmem_limit_bytes=VMEM_BYTES),
+        cost_estimate=pl.CostEstimate(flops=1 << 30, bytes_accessed=5 << 20, transcendentals=0),
+        name="add_halo",
+    )(main, above, below, rows, taps_across)
+
+
+def project_kernel(update_ref, weight_ref, sums_ref, out_ref):
+    total = (sums_ref[0, 0] + sums_ref[1, 0]) + (sums_ref[2, 0] + sums_ref[3, 0])
     weight = weight_ref[0]
     factor = weight / jnp.maximum(jnp.sqrt(total), weight)
     count = factor.shape[0]
@@ -451,18 +537,22 @@
 
 def project(update, weight, sums):
     bands, pixels, columns = update.shape
+    half = weight.shape[1]
     wide = pl.BlockSpec((1, pixels, columns), lambda i: (i, 0, 0))
-    narrow = pl.BlockSpec((1, weight.shape[1], columns), lambda i: (i, 0, 0))
     return pl.pallas_call(
         project_kernel,
         grid=(bands,),
-        in_specs=[wide] + [narrow] * 5,
+        in_specs=[
+            wide,
+            pl.BlockSpec((1, half, columns), lambda i: (i, 0, 0)),
+            pl.BlockSpec((sums.shape[0], 1, half, columns), lambda i: (0, i, 0, 0)),
+        ],
         out_specs=wide,
         out_shape=jax.ShapeDtypeStruct(update.shape, jnp.float32),
         compiler_params=pltpu.CompilerParams(vmem_limit_bytes=VMEM_BYTES),
         cost_estimate=pl.CostEstimate(flops=4 << 20, bytes_accessed=5 << 20, transcendentals=0),
         name="project",
-    )(update, weight, *sums)
+    )(update, weight, sums)
 
 
 def shards(
@@ -486,11 +576,12 @@
     )
     dual_here, _ = lax.optimization_barrier((dual, grid))
     base_a, base_b, to_above, to_below = synthesize(dual_here, primal)
-    from_above = lax.ppermute(to_below, "fac", forward)
-    from_below = lax.ppermute(to_above, "fac", backward)
-    by_facet, from_above, from_below = lax.optimization_barrier((by_facet, from_above, from_below))
-    base_a = add_sides(base_a, from_above, from_below)
-
+    near = [pair for pair in forward if pair[1] % RING != 0]
+    far = [pair for pair in forward if pair[1] % RING == 0]
+    turned = lambda those: [(b, a) for a, b in those]
+    far_sides = [lax.ppermute(to_below, "fac", far), lax.ppermute(to_above, "fac", turned(far))]
+    by_facet, to_above, to_below = lax.optimization_barrier((by_facet, to_above, to_below))
+    sides = [lax.ppermute(to_below, "fac", near), lax.ppermute(to_above, "fac", turned(near))]
     parts = by_facet.reshape(groups, channels, 2, half, quarter)
 
     def piece(part, step):
@@ -507,16 +598,14 @@
     core_b = lax.ppermute(sent_b, "chan", pairs(1))
     far_b = lax.ppermute(jnp.stack([kept_b, core_b[1]]), "chan", pairs(2))
     me = me.astype(jnp.int32).reshape(1)
-    image_a, first, last = update_border(me, base_a, parts, backs_a, primal)
+    image_a, first, last = update_border(
+        border_sum(me, add_sides(base_a, *far_sides), parts, backs_a), sides, primal
+    )
     above = lax.ppermute(last, "fac", forward)
     below = lax.ppermute(first, "fac", backward)
-    image, update, squares = finish(
-        me, image_a, base_b, parts, core_b, far_b, primal, above, below, dual
-    )
-    sums = [squares]
-    for step in range(1, groups):
-        pairs = [(i, i ^ step) for i in range(groups)]
-        sums.append(lax.ppermute(squares, "chan", pairs))
+    image, main = finish(me, image_a, base_b, parts, core_b, far_b, primal, dual)
+    update, squares = add_halo(main, above, below, half)
+    sums = lax.all_gather(squares, "chan")
     dual_next = project(update, l21_weight, sums)
     return (image.reshape(primal_image.shape), dual_next.reshape(dual_coef.shape))
 

time: 136 us -> 130 us (0.956)
  waiting for transfers between devices: 60.8 us -> 42.3 us
  blocking collectives: 0 us -> 8.41 us
  Pallas kernels: 26.2 us -> 29.6 us
    ppermute x5 -> x4, waiting for transfers between devices: 42.7 us -> 5.83 us  [the longest x1 3.26 us: shards(): lax.ppermute(to_above, 'fac', turned(near))]
    all_to_all x1, waiting for transfers between devices: 0.01 us -> 29.4 us  [shards(): lax.all_to_all(grid.reshape(facets, rows, quarter), 'fac', split_axis=0,...]
    all_gather x0 -> x1, blocking collectives: none -> 8.41 us  [shards(): sums = lax.all_gather(squares, 'chan')]
    ppermute x1, waiting for transfers between devices: 8.01 us -> 0.47 us  [shards(): above = lax.ppermute(last, 'fac', forward)]
    pallas_call x2 -> x4, Pallas kernels: 3.58 us -> 8.36 us  [the longest x1 3.77 us: add_halo(): pl.pallas_call(halo_kernel, grid=(blocks,), in_specs=[wide, pl.BlockSpec(...]
    ppermute x3, waiting for transfers between devices: 8.7 us -> 5.4 us  [shards(): lax.ppermute(sent_a[step - 1], 'chan', pairs(step))]
    unnamed x30 -> x32, local copies, waits for them, and re-layouts: 6.16 us -> 6.32 us
    ppermute x5 -> x4, starting transfers between devices: 12.2 us -> 12.2 us  [the longest x1 8.35 us: shards(): lax.ppermute(to_above, 'fac', turned(far))]
  transfers between devices with their start and end apart: 13 -> 12, of which waited for: 8 -> 6; matrix products, arithmetic and copies ran while one was open for 0% -> 0% of each run, Pallas kernels for 6% -> 12%
where the time goes in v2:
time: 130 us; the launch traced here: 128 us
  waiting for transfers between devices  42.3 us (33%)
  starting transfers between devices  40.5 us (31%)
  Pallas kernels  29.6 us (23%)
  blocking collectives  8.41 us (6%)
  local copies, waits for them, and re-layouts  6.7 us (5%)
    all_to_all x1, waiting for transfers between devices, shards(): lax.all_to_all(grid.reshape(facets, rows, quarter), 'fac', split_axis=0,...  29.4 us
    all_to_all x1, starting transfers between devices, shards(): lax.all_to_all(grid.reshape(facets, rows, quarter), 'fac', split_axis=0,...  13.2 us
    all_gather x1, blocking collectives, shards(): sums = lax.all_gather(squares, 'chan')  8.41 us
    ppermute x1, starting transfers between devices, shards(): lax.ppermute(to_above, 'fac', turned(far))  8.35 us
    pallas_call x1, Pallas kernels, back_project(): pl.pallas_call(functools.partial(back_kernel, rows=rows), in_specs=[vmem,...  8.3 us
    ppermute x1, starting transfers between devices, shards(): below = lax.ppermute(first, 'fac', backward)  6.93 us
    unnamed x32, local copies, waits for them, and re-layouts  6.32 us
    pallas_call x1, Pallas kernels, finish(): pl.pallas_call(finish_kernel, grid_spec=pltpu.PrefetchScalarGridSpec(num_...  6.24 us
  transfers between devices with their start and end apart: 12, of which 6 were waited for; matrix products, arithmetic and copies ran while one was open for 0% of the time, Pallas kernels for 12%

profile of v2, /device:TPU:8, one launch (start us, length us, event | category | flops | bytes accessed | tf_op | source)
XLA Modules:
  0.0 128.5 jit_solution(3563879501832014358)
XLA Ops:
  0.6 8.3 %back_project.1 = f32[1024,512]{1,0:T(8,128)} custom-call(bf16[1,4096]{1,0:T(2,128)(2,1)} %vis_ref.1, s32[1,4096]{1,0:T(1,128)} %tile_ref.1, bf16[4096,128]{1,0:T(8,128)(2,1)} %bitcast.36, s32[4096,128]{1,0:T(8,128)} %bitcast.35), custom_call_target="tpu_custom_call" | custom-call | flops 4294967296 | bytes 6291456 | tf_op jit(solution)/shard_map/back_project/pallas_call | solution.py:183
  8.9 0.0 copy-start.9
  9.0 13.2 %all-to-all-start = ((f32[64,16,512]{2,1,0:T(8,128)}), f32[64,16,512]{2,1,0:T(8,128)S(1)}, u32[]{:S(2)}, u32[]{:S(2)}) async-start(f32[64,16,512]{2,1,0:T(8,128)} %bitcast.33), calls=%async_computation | async-start | bytes 4194304 | tf_op jit(solution)/shard_map/all_to_all | solution.py:574
  22.1 0.0 copy-done.9
  22.2 0.0 copy-start
  22.2 1.6 %copy-done = f32[16,16,2048]{2,1,0:T(8,128)S(1)} copy-done((f32[16,16,2048]{2,1,0:T(8,128)S(1)}, f32[16,16,2048]{2,1,0:T(8,128)}, u32[]{:S(2)}) %copy-start) | copy-done | bytes 2097176
  23.7 0.0 copy-start.5
  23.8 1.6 %copy-done.5 = f32[4,16,8,1024]{3,2,1,0:T(8,128)S(1)} copy-done((f32[4,16,8,1024]{3,2,1,0:T(8,128)S(1)}, f32[4,16,8,1024]{3,2,1,0:T(8,128)}, u32[]{:S(2)}) %copy-start.5) | copy-done | bytes 2097176
  25.3 0.0 copy-start.7
  25.3 1.1 copy-done.7
  26.5 5.2 %synthesis.1 = (f32[128,2048]{1,0:T(8,128)S(1)}, f32[128,2048]{1,0:T(8,128)S(1)}, f32[48,2048]{1,0:T(8,128)S(1)}, f32[48,2048]{1,0:T(8,128)S(1)}) custom-call(f32[4,128,1024]{2,1,0:T(8,128)S(1)} %bitcast.30, f32[16,2,8,2048]{3,2,1,0:T(8,128)S(1)} %bitcast.27, bf16[2,352,256]{2,1,0:T(8,128)(2,1)S(1)} %copy-done.9, bf16[2,768,256]{2,1,0:T(8,128)(2,1)S(1)} %copy-done.7), custom_call_target="tpu_custom_call" | custom-call | flops 8589934592 | bytes 8388608 | tf_op jit(solution)/shard_map/synthesis/pallas_call | solution.py:245
  31.7 0.0 copy-start.12
  31.7 1.0 copy-done.12
  32.7 0.0 copy-start.14
  32.7 1.0 copy-done.14
  33.7 1.3 collective-permute-start
  34.9 8.3 %collective-permute-start.1 = (f32[48,2048]{1,0:T(8,128)S(1)}, f32[48,2048]{1,0:T(8,128)}, u32[]{:S(2)}, u32[]{:S(2)}) collective-permute-start(f32[48,2048]{1,0:T(8,128)S(1)} %get-tuple-element.31), channel_id=1, source_target_pairs={{32,28},{64,60},{96,92},{128,124},{160,156},{192,188},{224,220},{3... | collective-permute-start | bytes 1179656 | tf_op jit(solution)/shard_map/ppermute | solution.py:582
  43.3 29.4 %all-to-all-done = f32[64,16,512]{2,1,0:T(8,128)S(1)} async-done(((f32[64,16,512]{2,1,0:T(8,128)}), f32[64,16,512]{2,1,0:T(8,128)S(1)}, u32[]{:S(2)}, u32[]{:S(2)}) %all-to-all-start) | async-done | bytes 2097184 | tf_op jit(solution)/shard_map/all_to_all | solution.py:574
  72.7 0.2 fusion
  72.9 0.0 copy-start.3
  72.9 0.0 copy-start.15
  72.9 0.2 dynamic-slice_bitcast_fusion
  73.1 0.1 collective-permute-start.2
  73.2 2.8 %collective-permute-start.3 = (f32[128,512]{1,0:T(8,128)S(1)}, f32[128,512]{1,0:T(8,128)S(1)}, u32[]{:S(2)}, u32[]{:S(2)}) collective-permute-start(f32[128,512]{1,0:T(8,128)S(1)} %get-tuple-element.28), channel_id=1, source_target_pairs={{0,2},{1,3},{2,0},{3,1},{4,6},{5,7},{6,4},{7,5},{8,10},{9,11},{10,... | collective-permute-start | bytes 786440 | tf_op jit(solution)/shard_map/ppermute | solution.py:597
  76.0 0.6 collective-permute-start.4
  76.6 2.6 %collective-permute-done.above_ref = f32[48,2048]{1,0:T(8,128)S(1)} collective-permute-done((f32[48,2048]{1,0:T(8,128)S(1)}, f32[48,2048]{1,0:T(8,128)S(1)}, u32[]{:S(2)}, u32[]{:S(2)}) %collective-permute-start) | collective-permute-done | bytes 393248 | tf_op jit(solution)/shard_map/ppermute | solution.py:582
  79.1 0.0 collective-permute-start.7
  79.2 0.0 collective-permute-done.1.below_ref
  79.2 0.0 copy-done.3
  79.2 0.0 copy-done.15
  79.2 1.4 %add_sides.1.base_ref = f32[128,2048]{1,0:T(8,128)S(1)} custom-call(f32[128,2048]{1,0:T(8,128)S(1)} %copy-done.15, f32[48,2048]{1,0:T(8,128)S(1)} %collective-permute-done.above_ref, f32[48,2048]{1,0:T(8,128)} %collective-permute-done.1.below_ref, bf16[128,96]{1,0:T(8,128)(2,1)S(1)} %copy-done.3), custom_call_target="tpu_custom_call" | custom-call | flops 42949672960 | bytes 3145728 | tf_op jit(solution)/shard_map/add_sides/pallas_call | solution.py:270
  80.6 1.3 %collective-permute-start.5 = (f32[48,2048]{1,0:T(8,128)S(1)}, f32[48,2048]{1,0:T(8,128)S(1)}, u32[]{:S(2)}, u32[]{:S(2)}) collective-permute-start(f32[48,2048]{1,0:T(8,128)S(1)} %get-tuple-element.30), channel_id=1, source_target_pairs={{0,4},{4,8},{8,12},{12,16},{16,20},{20,24},{24,28},{32,36},{36,40}... | collective-permute-start | bytes 1179656 | tf_op jit(solution)/shard_map/ppermute | solution.py:584
  81.9 0.0 collective-permute-done.7.one_ref
  81.9 1.3 %collective-permute-start.6 = (f32[48,2048]{1,0:T(8,128)S(1)}, f32[48,2048]{1,0:T(8,128)S(1)}, u32[]{:S(2)}, u32[]{:S(2)}) collective-permute-start(f32[48,2048]{1,0:T(8,128)S(1)} %get-tuple-element.31), channel_id=1, source_target_pairs={{4,0},{8,4},{12,8},{16,12},{20,16},{24,20},{28,24},{36,32},{40,36}... | collective-permute-start | bytes 1179656 | tf_op jit(solution)/shard_map/ppermute | solution.py:584
  83.3 0.0 collective-permute-done.2.one_ref
  83.3 2.8 %collective-permute-start.8 = (f32[2,128,512]{2,1,0:T(8,128)S(1)}, f32[2,128,512]{2,1,0:T(8,128)S(1)}, u32[]{:S(2)}, u32[]{:S(2)}) collective-permute-start(f32[2,128,512]{2,1,0:T(8,128)S(1)} %pad_maximum_fusion.1), channel_id=1, source_target_pairs={{0,2},{1,3},{2,0},{3,1},{4,6},{5,7},{6,4},{7,5},{8,10},{9,11},{10,... | collective-permute-start | bytes 1572872 | tf_op jit(solution)/shard_map/ppermute | solution.py:599
  86.1 0.0 collective-permute-done.3.two_ref
  86.1 5.4 %collective-permute-done.4.three_ref = f32[128,512]{1,0:T(8,128)S(1)} collective-permute-done((f32[128,512]{1,0:T(8,128)S(1)}, f32[128,512]{1,0:T(8,128)S(1)}, u32[]{:S(2)}, u32[]{:S(2)}) %collective-permute-start.4) | collective-permute-done | bytes 262176 | tf_op jit(solution)/shard_map/ppermute | solution.py:597
  91.5 0.5 border_sum.1.base_ref
  92.0 0.0 copy-start.6
  92.0 0.0 copy-start.8
  92.1 0.0 copy-start.10
  92.1 0.0 copy-start.13
  92.1 0.0 collective-permute-done.5.above_ref
  92.1 3.3 %collective-permute-done.6.below_ref = f32[48,2048]{1,0:T(8,128)S(1)} collective-permute-done((f32[48,2048]{1,0:T(8,128)S(1)}, f32[48,2048]{1,0:T(8,128)S(1)}, u32[]{:S(2)}, u32[]{:S(2)}) %collective-permute-start.6) | collective-permute-done | bytes 393248 | tf_op jit(solution)/shard_map/ppermute | solution.py:584
  95.3 0.0 copy-done.1
  95.4 0.0 copy-done.4
  95.4 2.2 %update_border.1 = (f32[128,2048]{1,0:T(8,128)S(1)}, f32[48,2048]{1,0:T(8,128)S(1)}, f32[48,2048]{1,0:T(8,128)S(1)}) custom-call(f32[128,2048]{1,0:T(8,128)S(1)} %border_sum.1.base_ref, f32[48,2048]{1,0:T(8,128)S(1)} %collective-permute-done.5.above_ref, f32[48,2048]{1,0:T(8,128)S(1)} %collective-permute-done.6.below_ref, f32[16,2,8,2048]{3,2,1,0:T(8,128)S(1)} %bitcast.28, ...), custom_call_target="tpu_custom_call" | custom-call | flops 4194304 | bytes 4194304 | tf_op jit(solution)/shard_map/update_border/pallas_call | solution.py:333
  97.6 1.9 %collective-permute-start.9 = (f32[48,2048]{1,0:T(8,128)S(1)}, f32[48,2048]{1,0:T(8,128)S(1)}, u32[]{:S(2)}, u32[]{:S(2)}) collective-permute-start(f32[48,2048]{1,0:T(8,128)S(1)} %get-tuple-element.38), channel_id=1, source_target_pairs={{0,4},{4,8},{8,12},{12,16},{16,20},{20,24},{24,28},{28,32},{32,36}... | collective-permute-start | bytes 1179656 | tf_op jit(solution)/shard_map/ppermute | solution.py:604
  99.5 6.9 %collective-permute-start.10 = (f32[48,2048]{1,0:T(8,128)S(1)}, f32[48,2048]{1,0:T(8,128)S(1)}, u32[]{:S(2)}, u32[]{:S(2)}) collective-permute-start(f32[48,2048]{1,0:T(8,128)S(1)} %get-tuple-element.39), channel_id=1, source_target_pairs={{4,0},{8,4},{12,8},{16,12},{20,16},{24,20},{28,24},{32,28},{36,32}... | collective-permute-start | bytes 1179656 | tf_op jit(solution)/shard_map/ppermute | solution.py:605
  106.4 0.0 collective-permute-done.8.two_ref.three_ref
  106.4 0.0 copy-done.6
  106.4 0.0 copy-done.8
  106.5 0.0 copy-done.10
  106.5 0.0 copy-done.13
  106.5 0.0 copy-start.11
  106.5 6.2 %finish.1 = (f32[16,2,8,2048]{3,2,1,0:T(8,128)}, f32[4,128,1024]{2,1,0:T(8,128)S(1)}) custom-call(s32[1]{0:T(128)} %bitcast.me_ref, f32[128,2048]{1,0:T(8,128)S(1)} %get-tuple-element.32.image_a_ref, f32[128,2048]{1,0:T(8,128)S(1)} %copy-done.13, f32[4,16,2,8,512]{4,3,2,1,0:T(8,128)S(1)} %bitcast.25, f32[2,128,512]{2,1,0:T(8,128)S(1)} %collective-permute-done.7.one_ref, ...), custom_call_target="tpu_custom_call" | custom-call | flops 4294967296 | bytes 12582912 | tf_op jit(solution)/shard_map/finish/pallas_call | solution.py:425
  112.7 0.5 collective-permute-done.9.above_ref
  113.2 1.2 collective-permute-done.10.below_ref
  114.4 0.0 copy-done.11
  114.4 3.8 %add_halo.1 = (f32[4,128,1024]{2,1,0:T(8,128)S(1)}, f32[4,8,1024]{2,1,0:T(8,128)S(1)}) custom-call(f32[4,128,1024]{2,1,0:T(8,128)S(1)} %get-tuple-element.37.main_ref, f32[48,2048]{1,0:T(8,128)S(1)} %collective-permute-done.9.above_ref, f32[48,2048]{1,0:T(8,128)S(1)} %collective-permute-done.10.below_ref, bf16[2,256,96]{2,1,0:T(8,128)(2,1)S(1)} %copy-done.11, ...), custom_call_target="tpu_custom_call" | custom-call | flops 1073741824 | bytes 5242880 | tf_op jit(solution)/shard_map/add_halo/pallas_call | solution.py:506
  118.2 8.4 %all-gather = f32[16,8,1024]{2,1,0:T(8,128)S(1)} all-gather(f32[4,8,1024]{2,1,0:T(8,128)S(1)} %get-tuple-element.41), channel_id=2, replica_groups=mesh['fac'=64,'chan'=4] {'chan'}, dimensions={0}, use_global_device_ids=true | all-gather | bytes 655360 | tf_op jit(solution)/shard_map/all_gather | solution.py:608
  126.6 0.0 copy-done.2
  126.6 1.9 %project.1 = f32[4,128,1024]{2,1,0:T(8,128)} custom-call(f32[4,128,1024]{2,1,0:T(8,128)S(1)} %get-tuple-element.40.update_ref, f32[4,8,1024]{2,1,0:T(8,128)S(1)} %copy-done.2, f32[4,4,8,1024]{3,2,1,0:T(8,128)S(1)} %bitcast.26), custom_call_target="tpu_custom_call" | custom-call | flops 4194304 | bytes 5242880 | tf_op jit(solution)/shard_map/project/pallas_call | solution.py:542
  (6 shorter events, 0.1 us)
Async XLA Ops:
  8.9 13.2 %copy-start.9 = (bf16[2,352,256]{2,1,0:T(8,128)(2,1)S(1)}, bf16[2,352,256]{2,1,0:T(8,128)(2,1)}, u32[]{:S(2)}) copy-start(bf16[2,352,256]{2,1,0:T(8,128)(2,1)} %constant.46.clone.rows_ref) | copy-start | bytes 1081348
  9.0 63.7 %all-to-all-start = ((f32[64,16,512]{2,1,0:T(8,128)}), f32[64,16,512]{2,1,0:T(8,128)S(1)}, u32[]{:S(2)}, u32[]{:S(2)}) async-start(f32[64,16,512]{2,1,0:T(8,128)} %bitcast.33), calls=%async_computation | async-start | bytes 4194304 | tf_op jit(solution)/shard_map/all_to_all | solution.py:574
  22.2 1.6 %copy-start = (f32[16,16,2048]{2,1,0:T(8,128)S(1)}, f32[16,16,2048]{2,1,0:T(8,128)}, u32[]{:S(2)}) copy-start(f32[16,16,2048]{2,1,0:T(8,128)} %param.16) | copy-start | bytes 6291460
  23.7 1.6 %copy-start.5 = (f32[4,16,8,1024]{3,2,1,0:T(8,128)S(1)}, f32[4,16,8,1024]{3,2,1,0:T(8,128)}, u32[]{:S(2)}) copy-start(f32[4,16,8,1024]{3,2,1,0:T(8,128)} %param.17) | copy-start | bytes 6291460
  25.3 1.1 copy-start.7
  31.7 1.0 copy-start.12
  32.7 1.0 copy-start.14
  33.7 45.5 %collective-permute-start = (f32[48,2048]{1,0:T(8,128)S(1)}, f32[48,2048]{1,0:T(8,128)S(1)}, u32[]{:S(2)}, u32[]{:S(2)}) collective-permute-start(f32[48,2048]{1,0:T(8,128)S(1)} %get-tuple-element.30), channel_id=1, source_target_pairs={{28,32},{60,64},{92,96},{124,128},{156,160},{188,192},{220,224},{2... | collective-permute-start | bytes 1179656 | tf_op jit(solution)/shard_map/ppermute | solution.py:582
  34.9 44.2 %collective-permute-start.1 = (f32[48,2048]{1,0:T(8,128)S(1)}, f32[48,2048]{1,0:T(8,128)}, u32[]{:S(2)}, u32[]{:S(2)}) collective-permute-start(f32[48,2048]{1,0:T(8,128)S(1)} %get-tuple-element.31), channel_id=1, source_target_pairs={{32,28},{64,60},{96,92},{128,124},{160,156},{192,188},{224,220},{3... | collective-permute-start | bytes 1179656 | tf_op jit(solution)/shard_map/ppermute | solution.py:582
  72.9 6.3 %copy-start.3 = (bf16[128,96]{1,0:T(8,128)(2,1)S(1)}, bf16[128,96]{1,0:T(8,128)(2,1)}, u32[]{:S(2)}) copy-start(bf16[128,96]{1,0:T(8,128)(2,1)} %constant.48.clone.place_ref) | copy-start | bytes 73732
  72.9 6.3 %copy-start.15 = (f32[128,2048]{1,0:T(8,128)S(1)}, f32[128,2048]{1,0:T(8,128)}, u32[]{:S(2)}) copy-start(f32[128,2048]{1,0:T(8,128)} %copy-done.14) | copy-start | bytes 3145732
  73.1 10.2 %collective-permute-start.2 = (f32[128,512]{1,0:T(8,128)S(1)}, f32[128,512]{1,0:T(8,128)S(1)}, u32[]{:S(2)}, u32[]{:S(2)}) collective-permute-start(f32[128,512]{1,0:T(8,128)S(1)} %get-tuple-element.27), channel_id=1, source_target_pairs={{0,1},{1,0},{2,3},{3,2},{4,5},{5,4},{6,7},{7,6},{8,9},{9,8},{10,11... | collective-permute-start | bytes 786440 | tf_op jit(solution)/shard_map/ppermute | solution.py:597
  73.2 12.9 %collective-permute-start.3 = (f32[128,512]{1,0:T(8,128)S(1)}, f32[128,512]{1,0:T(8,128)S(1)}, u32[]{:S(2)}, u32[]{:S(2)}) collective-permute-start(f32[128,512]{1,0:T(8,128)S(1)} %get-tuple-element.28), channel_id=1, source_target_pairs={{0,2},{1,3},{2,0},{3,1},{4,6},{5,7},{6,4},{7,5},{8,10},{9,11},{10,... | collective-permute-start | bytes 786440 | tf_op jit(solution)/shard_map/ppermute | solution.py:597
  76.0 15.5 %collective-permute-start.4 = (f32[128,512]{1,0:T(8,128)S(1)}, f32[128,512]{1,0:T(8,128)S(1)}, u32[]{:S(2)}, u32[]{:S(2)}) collective-permute-start(f32[128,512]{1,0:T(8,128)S(1)} %get-tuple-element.29), channel_id=1, source_target_pairs={{0,3},{1,2},{2,1},{3,0},{4,7},{5,6},{6,5},{7,4},{8,11},{9,10},{10,... | collective-permute-start | bytes 786440 | tf_op jit(solution)/shard_map/ppermute | solution.py:597
  79.1 2.8 %collective-permute-start.7 = (f32[2,128,512]{2,1,0:T(8,128)S(1)}, f32[2,128,512]{2,1,0:T(8,128)S(1)}, u32[]{:S(2)}, u32[]{:S(2)}) collective-permute-start(f32[2,128,512]{2,1,0:T(8,128)S(1)} %pad_maximum_fusion), channel_id=1, source_target_pairs={{0,1},{1,0},{2,3},{3,2},{4,5},{5,4},{6,7},{7,6},{8,9},{9,8},{10,11... | collective-permute-start | bytes 1572872 | tf_op jit(solution)/shard_map/ppermute | solution.py:598
  80.6 11.5 %collective-permute-start.5 = (f32[48,2048]{1,0:T(8,128)S(1)}, f32[48,2048]{1,0:T(8,128)S(1)}, u32[]{:S(2)}, u32[]{:S(2)}) collective-permute-start(f32[48,2048]{1,0:T(8,128)S(1)} %get-tuple-element.30), channel_id=1, source_target_pairs={{0,4},{4,8},{8,12},{12,16},{16,20},{20,24},{24,28},{32,36},{36,40}... | collective-permute-start | bytes 1179656 | tf_op jit(solution)/shard_map/ppermute | solution.py:584
  81.9 13.4 %collective-permute-start.6 = (f32[48,2048]{1,0:T(8,128)S(1)}, f32[48,2048]{1,0:T(8,128)S(1)}, u32[]{:S(2)}, u32[]{:S(2)}) collective-permute-start(f32[48,2048]{1,0:T(8,128)S(1)} %get-tuple-element.31), channel_id=1, source_target_pairs={{4,0},{8,4},{12,8},{16,12},{20,16},{24,20},{28,24},{36,32},{40,36}... | collective-permute-start | bytes 1179656 | tf_op jit(solution)/shard_map/ppermute | solution.py:584
  83.3 23.1 %collective-permute-start.8 = (f32[2,128,512]{2,1,0:T(8,128)S(1)}, f32[2,128,512]{2,1,0:T(8,128)S(1)}, u32[]{:S(2)}, u32[]{:S(2)}) collective-permute-start(f32[2,128,512]{2,1,0:T(8,128)S(1)} %pad_maximum_fusion.1), channel_id=1, source_target_pairs={{0,2},{1,3},{2,0},{3,1},{4,6},{5,7},{6,4},{7,5},{8,10},{9,11},{10,... | collective-permute-start | bytes 1572872 | tf_op jit(solution)/shard_map/ppermute | solution.py:599
  91.5 3.8 %copy-start.1 = (f32[16,16,2048]{2,1,0:T(8,128)S(1)}, f32[16,16,2048]{2,1,0:T(8,128)}, u32[]{:S(2)}) copy-start(f32[16,16,2048]{2,1,0:T(8,128)} %param.16) | copy-start | bytes 6291460
  91.5 3.8 %copy-start.4 = (bf16[96,128]{1,0:T(8,128)(2,1)S(1)}, bf16[96,128]{1,0:T(8,128)(2,1)}, u32[]{:S(2)}) copy-start(bf16[96,128]{1,0:T(8,128)(2,1)} %constant.49.clone.pick_ref) | copy-start | bytes 73732
  92.0 14.4 %copy-start.6 = (f32[4,16,8,1024]{3,2,1,0:T(8,128)S(1)}, f32[4,16,8,1024]{3,2,1,0:T(8,128)}, u32[]{:S(2)}) copy-start(f32[4,16,8,1024]{3,2,1,0:T(8,128)} %param.17) | copy-start | bytes 6291460
  92.0 14.4 %copy-start.8 = (bf16[2,512,256]{2,1,0:T(8,128)(2,1)S(1)}, bf16[2,512,256]{2,1,0:T(8,128)(2,1)}, u32[]{:S(2)}) copy-start(bf16[2,512,256]{2,1,0:T(8,128)(2,1)} %constant.51.clone.columns_ref) | copy-start | bytes 1572868
  92.1 14.4 %copy-start.10 = (bf16[2,256,256]{2,1,0:T(8,128)(2,1)S(1)}, bf16[2,256,256]{2,1,0:T(8,128)(2,1)}, u32[]{:S(2)}) copy-start(bf16[2,256,256]{2,1,0:T(8,128)(2,1)} %constant.50.clone.rows_ref) | copy-start | bytes 786436
  92.1 14.4 %copy-start.13 = (f32[128,2048]{1,0:T(8,128)S(1)}, f32[128,2048]{1,0:T(8,128)}, u32[]{:S(2)}) copy-start(f32[128,2048]{1,0:T(8,128)} %copy-done.12) | copy-start | bytes 3145732
  97.6 15.6 %collective-permute-start.9 = (f32[48,2048]{1,0:T(8,128)S(1)}, f32[48,2048]{1,0:T(8,128)S(1)}, u32[]{:S(2)}, u32[]{:S(2)}) collective-permute-start(f32[48,2048]{1,0:T(8,128)S(1)} %get-tuple-element.38), channel_id=1, source_target_pairs={{0,4},{4,8},{8,12},{12,16},{16,20},{20,24},{24,28},{28,32},{32,36}... | collective-permute-start | bytes 1179656 | tf_op jit(solution)/shard_map/ppermute | solution.py:604
  99.5 14.9 %collective-permute-start.10 = (f32[48,2048]{1,0:T(8,128)S(1)}, f32[48,2048]{1,0:T(8,128)S(1)}, u32[]{:S(2)}, u32[]{:S(2)}) collective-permute-start(f32[48,2048]{1,0:T(8,128)S(1)} %get-tuple-element.39), channel_id=1, source_target_pairs={{4,0},{8,4},{12,8},{16,12},{20,16},{24,20},{28,24},{32,28},{36,32}... | collective-permute-start | bytes 1179656 | tf_op jit(solution)/shard_map/ppermute | solution.py:605
  106.5 7.9 %copy-start.11 = (bf16[2,256,96]{2,1,0:T(8,128)(2,1)S(1)}, bf16[2,256,96]{2,1,0:T(8,128)(2,1)}, u32[]{:S(2)}) copy-start(bf16[2,256,96]{2,1,0:T(8,128)(2,1)} %constant.52.clone.rows_ref) | copy-start | bytes 294916
  114.4 12.2 %copy-start.2 = (f32[4,8,1024]{2,1,0:T(8,128)S(1)}, f32[4,8,1024]{2,1,0:T(8,128)}, u32[]{:S(2)}) copy-start(f32[4,8,1024]{2,1,0:T(8,128)} %weight_ref.1) | copy-start | bytes 393220

commit v3 on v2

--- a/solution.py
+++ b/solution.py
@@ -301,7 +301,7 @@
         ),
         out_shape=jax.ShapeDtypeStruct(base.shape, jnp.float32),
         compiler_params=pltpu.CompilerParams(vmem_limit_bytes=VMEM_BYTES),
-        cost_estimate=pl.CostEstimate(flops=20 << 30, bytes_accessed=3 << 20, transcendentals=0),
+        cost_estimate=pl.CostEstimate(flops=6 << 30, bytes_accessed=3 << 20, transcendentals=0),
         name="border_sum",
     )(me, base, parts, *backs)
 
@@ -323,7 +323,7 @@
 def update_border(base, sides, primal):
     pixels, columns = base.shape
     channels, _, half, _ = primal.shape
-    blocks = 4
+    blocks = 2
     width = columns // blocks
     pick = border_rows(channels, 2 * half)
     block = pl.BlockSpec((pixels, width), lambda i: (0, i))
@@ -499,7 +499,7 @@
     channels = pixels // half
     rows = split_constant(analysis_rows(channels, 2 * half)[:, 2 * pixels :])
     taps_across = split_constant(analysis_columns())
-    blocks = 4
+    blocks = 2
     wide = pl.BlockSpec((4, pixels, columns // blocks), lambda i: (0, 0, i))
     whole = lambda i: (0, 0)
     whole3 = lambda i: (0, 0, 0)

time: 130 us -> 129 us (level)
  no operation moved by 1% of the time
where the time goes in v3:
time: 129 us; the launch traced here: 127 us
  waiting for transfers between devices  42.3 us (33%)
  starting transfers between devices  40.5 us (31%)
  Pallas kernels  28.5 us (22%)
  blocking collectives  8.41 us (7%)
  local copies, waits for them, and re-layouts  6.7 us (5%)
    all_to_all x1, waiting for transfers between devices, shards(): lax.all_to_all(grid.reshape(facets, rows, quarter), 'fac', split_axis=0,...  29.4 us
    all_to_all x1, starting transfers between devices, shards(): lax.all_to_all(grid.reshape(facets, rows, quarter), 'fac', split_axis=0,...  13.2 us
    all_gather x1, blocking collectives, shards(): sums = lax.all_gather(squares, 'chan')  8.41 us
    ppermute x1, starting transfers between devices, shards(): lax.ppermute(to_above, 'fac', turned(far))  8.35 us
    pallas_call x1, Pallas kernels, back_project(): pl.pallas_call(functools.partial(back_kernel, rows=rows), in_specs=[vmem,...  8.3 us
    ppermute x1, starting transfers between devices, shards(): below = lax.ppermute(first, 'fac', backward)  6.93 us
    unnamed x32, local copies, waits for them, and re-layouts  6.32 us
    pallas_call x1, Pallas kernels, finish(): pl.pallas_call(finish_kernel, grid_spec=pltpu.PrefetchScalarGridSpec(num_...  6.23 us
  transfers between devices with their start and end apart: 12, of which 6 were waited for; matrix products, arithmetic and copies ran while one was open for 0% of the time, Pallas kernels for 12%

profile of v3, /device:TPU:8, one launch (start us, length us, event | category | flops | bytes accessed | tf_op | source)
XLA Modules:
  0.0 127.4 jit_solution(12815606094946507576)
XLA Ops:
  0.6 8.3 %back_project.1 = f32[1024,512]{1,0:T(8,128)} custom-call(bf16[1,4096]{1,0:T(2,128)(2,1)} %vis_ref.1, s32[1,4096]{1,0:T(1,128)} %tile_ref.1, bf16[4096,128]{1,0:T(8,128)(2,1)} %bitcast.36, s32[4096,128]{1,0:T(8,128)} %bitcast.35), custom_call_target="tpu_custom_call" | custom-call | flops 4294967296 | bytes 6291456 | tf_op jit(solution)/shard_map/back_project/pallas_call | solution.py:183
  8.9 0.0 copy-start.9
  9.0 13.2 %all-to-all-start = ((f32[64,16,512]{2,1,0:T(8,128)}), f32[64,16,512]{2,1,0:T(8,128)S(1)}, u32[]{:S(2)}, u32[]{:S(2)}) async-start(f32[64,16,512]{2,1,0:T(8,128)} %bitcast.33), calls=%async_computation | async-start | bytes 4194304 | tf_op jit(solution)/shard_map/all_to_all | solution.py:574
  22.1 0.0 copy-done.9
  22.2 0.0 copy-start
  22.2 1.6 %copy-done = f32[16,16,2048]{2,1,0:T(8,128)S(1)} copy-done((f32[16,16,2048]{2,1,0:T(8,128)S(1)}, f32[16,16,2048]{2,1,0:T(8,128)}, u32[]{:S(2)}) %copy-start) | copy-done | bytes 2097176
  23.7 0.0 copy-start.5
  23.8 1.6 %copy-done.5 = f32[4,16,8,1024]{3,2,1,0:T(8,128)S(1)} copy-done((f32[4,16,8,1024]{3,2,1,0:T(8,128)S(1)}, f32[4,16,8,1024]{3,2,1,0:T(8,128)}, u32[]{:S(2)}) %copy-start.5) | copy-done | bytes 2097176
  25.3 0.0 copy-start.7
  25.3 1.1 copy-done.7
  26.5 5.2 %synthesis.1 = (f32[128,2048]{1,0:T(8,128)S(1)}, f32[128,2048]{1,0:T(8,128)S(1)}, f32[48,2048]{1,0:T(8,128)S(1)}, f32[48,2048]{1,0:T(8,128)S(1)}) custom-call(f32[4,128,1024]{2,1,0:T(8,128)S(1)} %bitcast.30, f32[16,2,8,2048]{3,2,1,0:T(8,128)S(1)} %bitcast.27, bf16[2,352,256]{2,1,0:T(8,128)(2,1)S(1)} %copy-done.9, bf16[2,768,256]{2,1,0:T(8,128)(2,1)S(1)} %copy-done.7), custom_call_target="tpu_custom_call" | custom-call | flops 8589934592 | bytes 8388608 | tf_op jit(solution)/shard_map/synthesis/pallas_call | solution.py:245
  31.7 0.0 copy-start.12
  31.7 1.0 copy-done.12
  32.7 0.0 copy-start.14
  32.7 1.0 copy-done.14
  33.7 1.3 %collective-permute-start = (f32[48,2048]{1,0:T(8,128)S(1)}, f32[48,2048]{1,0:T(8,128)S(1)}, u32[]{:S(2)}, u32[]{:S(2)}) collective-permute-start(f32[48,2048]{1,0:T(8,128)S(1)} %get-tuple-element.30), channel_id=1, source_target_pairs={{28,32},{60,64},{92,96},{124,128},{156,160},{188,192},{220,224},{2... | collective-permute-start | bytes 1179656 | tf_op jit(solution)/shard_map/ppermute | solution.py:582
  34.9 8.3 %collective-permute-start.1 = (f32[48,2048]{1,0:T(8,128)S(1)}, f32[48,2048]{1,0:T(8,128)}, u32[]{:S(2)}, u32[]{:S(2)}) collective-permute-start(f32[48,2048]{1,0:T(8,128)S(1)} %get-tuple-element.31), channel_id=1, source_target_pairs={{32,28},{64,60},{96,92},{128,124},{160,156},{192,188},{224,220},{3... | collective-permute-start | bytes 1179656 | tf_op jit(solution)/shard_map/ppermute | solution.py:582
  43.3 29.4 %all-to-all-done = f32[64,16,512]{2,1,0:T(8,128)S(1)} async-done(((f32[64,16,512]{2,1,0:T(8,128)}), f32[64,16,512]{2,1,0:T(8,128)S(1)}, u32[]{:S(2)}, u32[]{:S(2)}) %all-to-all-start) | async-done | bytes 2097184 | tf_op jit(solution)/shard_map/all_to_all | solution.py:574
  72.7 0.2 fusion
  72.9 0.0 copy-start.3
  72.9 0.0 copy-start.15
  72.9 0.2 dynamic-slice_bitcast_fusion
  73.1 0.1 collective-permute-start.2
  73.2 2.8 %collective-permute-start.3 = (f32[128,512]{1,0:T(8,128)S(1)}, f32[128,512]{1,0:T(8,128)S(1)}, u32[]{:S(2)}, u32[]{:S(2)}) collective-permute-start(f32[128,512]{1,0:T(8,128)S(1)} %get-tuple-element.28), channel_id=1, source_target_pairs={{0,2},{1,3},{2,0},{3,1},{4,6},{5,7},{6,4},{7,5},{8,10},{9,11},{10,... | collective-permute-start | bytes 786440 | tf_op jit(solution)/shard_map/ppermute | solution.py:597
  76.0 0.6 collective-permute-start.4
  76.6 2.6 %collective-permute-done.above_ref = f32[48,2048]{1,0:T(8,128)S(1)} collective-permute-done((f32[48,2048]{1,0:T(8,128)S(1)}, f32[48,2048]{1,0:T(8,128)S(1)}, u32[]{:S(2)}, u32[]{:S(2)}) %collective-permute-start) | collective-permute-done | bytes 393248 | tf_op jit(solution)/shard_map/ppermute | solution.py:582
  79.1 0.0 collective-permute-start.7
  79.2 0.0 collective-permute-done.1.below_ref
  79.2 0.0 copy-done.3
  79.2 0.0 copy-done.15
  79.2 1.4 %add_sides.1.base_ref = f32[128,2048]{1,0:T(8,128)S(1)} custom-call(f32[128,2048]{1,0:T(8,128)S(1)} %copy-done.15, f32[48,2048]{1,0:T(8,128)S(1)} %collective-permute-done.above_ref, f32[48,2048]{1,0:T(8,128)} %collective-permute-done.1.below_ref, bf16[128,96]{1,0:T(8,128)(2,1)S(1)} %copy-done.3), custom_call_target="tpu_custom_call" | custom-call | flops 42949672960 | bytes 3145728 | tf_op jit(solution)/shard_map/add_sides/pallas_call | solution.py:270
  80.6 1.3 %collective-permute-start.5 = (f32[48,2048]{1,0:T(8,128)S(1)}, f32[48,2048]{1,0:T(8,128)S(1)}, u32[]{:S(2)}, u32[]{:S(2)}) collective-permute-start(f32[48,2048]{1,0:T(8,128)S(1)} %get-tuple-element.30), channel_id=1, source_target_pairs={{0,4},{4,8},{8,12},{12,16},{16,20},{20,24},{24,28},{32,36},{36,40}... | collective-permute-start | bytes 1179656 | tf_op jit(solution)/shard_map/ppermute | solution.py:584
  81.9 0.0 collective-permute-done.7.one_ref
  81.9 1.3 %collective-permute-start.6 = (f32[48,2048]{1,0:T(8,128)S(1)}, f32[48,2048]{1,0:T(8,128)S(1)}, u32[]{:S(2)}, u32[]{:S(2)}) collective-permute-start(f32[48,2048]{1,0:T(8,128)S(1)} %get-tuple-element.31), channel_id=1, source_target_pairs={{4,0},{8,4},{12,8},{16,12},{20,16},{24,20},{28,24},{36,32},{40,36}... | collective-permute-start | bytes 1179656 | tf_op jit(solution)/shard_map/ppermute | solution.py:584
  83.3 0.0 collective-permute-done.2.one_ref
  83.3 2.8 %collective-permute-start.8 = (f32[2,128,512]{2,1,0:T(8,128)S(1)}, f32[2,128,512]{2,1,0:T(8,128)S(1)}, u32[]{:S(2)}, u32[]{:S(2)}) collective-permute-start(f32[2,128,512]{2,1,0:T(8,128)S(1)} %pad_maximum_fusion.1), channel_id=1, source_target_pairs={{0,2},{1,3},{2,0},{3,1},{4,6},{5,7},{6,4},{7,5},{8,10},{9,11},{10,... | collective-permute-start | bytes 1572872 | tf_op jit(solution)/shard_map/ppermute | solution.py:599
  86.1 0.0 collective-permute-done.3.two_ref
  86.1 5.4 %collective-permute-done.4.three_ref = f32[128,512]{1,0:T(8,128)S(1)} collective-permute-done((f32[128,512]{1,0:T(8,128)S(1)}, f32[128,512]{1,0:T(8,128)S(1)}, u32[]{:S(2)}, u32[]{:S(2)}) %collective-permute-start.4) | collective-permute-done | bytes 262176 | tf_op jit(solution)/shard_map/ppermute | solution.py:597
  91.5 0.5 border_sum.1.base_ref
  92.0 0.0 copy-start.6
  92.0 0.0 copy-start.8
  92.1 0.0 copy-start.10
  92.1 0.0 copy-start.13
  92.1 0.0 collective-permute-done.5.above_ref
  92.1 3.3 %collective-permute-done.6.below_ref = f32[48,2048]{1,0:T(8,128)S(1)} collective-permute-done((f32[48,2048]{1,0:T(8,128)S(1)}, f32[48,2048]{1,0:T(8,128)S(1)}, u32[]{:S(2)}, u32[]{:S(2)}) %collective-permute-start.6) | collective-permute-done | bytes 393248 | tf_op jit(solution)/shard_map/ppermute | solution.py:584
  95.3 0.0 copy-done.1
  95.4 0.0 copy-done.4
  95.4 1.6 %update_border.1 = (f32[128,2048]{1,0:T(8,128)S(1)}, f32[48,2048]{1,0:T(8,128)S(1)}, f32[48,2048]{1,0:T(8,128)S(1)}) custom-call(f32[128,2048]{1,0:T(8,128)S(1)} %border_sum.1.base_ref, f32[48,2048]{1,0:T(8,128)S(1)} %collective-permute-done.5.above_ref, f32[48,2048]{1,0:T(8,128)S(1)} %collective-permute-done.6.below_ref, f32[16,2,8,2048]{3,2,1,0:T(8,128)S(1)} %bitcast.28, ...), custom_call_target="tpu_custom_call" | custom-call | flops 4194304 | bytes 4194304 | tf_op jit(solution)/shard_map/update_border/pallas_call | solution.py:333
  97.0 1.9 %collective-permute-start.9 = (f32[48,2048]{1,0:T(8,128)S(1)}, f32[48,2048]{1,0:T(8,128)S(1)}, u32[]{:S(2)}, u32[]{:S(2)}) collective-permute-start(f32[48,2048]{1,0:T(8,128)S(1)} %get-tuple-element.38), channel_id=1, source_target_pairs={{0,4},{4,8},{8,12},{12,16},{16,20},{20,24},{24,28},{28,32},{32,36}... | collective-permute-start | bytes 1179656 | tf_op jit(solution)/shard_map/ppermute | solution.py:604
  98.9 6.9 %collective-permute-start.10 = (f32[48,2048]{1,0:T(8,128)S(1)}, f32[48,2048]{1,0:T(8,128)S(1)}, u32[]{:S(2)}, u32[]{:S(2)}) collective-permute-start(f32[48,2048]{1,0:T(8,128)S(1)} %get-tuple-element.39), channel_id=1, source_target_pairs={{4,0},{8,4},{12,8},{16,12},{20,16},{24,20},{28,24},{32,28},{36,32}... | collective-permute-start | bytes 1179656 | tf_op jit(solution)/shard_map/ppermute | solution.py:605
  105.8 0.0 collective-permute-done.8.two_ref.three_ref
  105.8 0.0 copy-done.6
  105.9 0.0 copy-done.8
  105.9 0.0 copy-done.10
  105.9 0.0 copy-done.13
  105.9 0.0 copy-start.11
  105.9 6.2 %finish.1 = (f32[16,2,8,2048]{3,2,1,0:T(8,128)}, f32[4,128,1024]{2,1,0:T(8,128)S(1)}) custom-call(s32[1]{0:T(128)} %bitcast.me_ref, f32[128,2048]{1,0:T(8,128)S(1)} %get-tuple-element.32.image_a_ref, f32[128,2048]{1,0:T(8,128)S(1)} %copy-done.13, f32[4,16,2,8,512]{4,3,2,1,0:T(8,128)S(1)} %bitcast.25, f32[2,128,512]{2,1,0:T(8,128)S(1)} %collective-permute-done.7.one_ref, ...), custom_call_target="tpu_custom_call" | custom-call | flops 4294967296 | bytes 12582912 | tf_op jit(solution)/shard_map/finish/pallas_call | solution.py:425
  112.1 0.5 collective-permute-done.9.above_ref
  112.6 1.2 collective-permute-done.10.below_ref
  113.8 0.0 copy-done.11
  113.8 3.3 %add_halo.1 = (f32[4,128,1024]{2,1,0:T(8,128)S(1)}, f32[4,8,1024]{2,1,0:T(8,128)S(1)}) custom-call(f32[4,128,1024]{2,1,0:T(8,128)S(1)} %get-tuple-element.37.main_ref, f32[48,2048]{1,0:T(8,128)S(1)} %collective-permute-done.9.above_ref, f32[48,2048]{1,0:T(8,128)S(1)} %collective-permute-done.10.below_ref, bf16[2,256,96]{2,1,0:T(8,128)(2,1)S(1)} %copy-done.11, ...), custom_call_target="tpu_custom_call" | custom-call | flops 1073741824 | bytes 5242880 | tf_op jit(solution)/shard_map/add_halo/pallas_call | solution.py:506
  117.1 8.4 %all-gather = f32[16,8,1024]{2,1,0:T(8,128)S(1)} all-gather(f32[4,8,1024]{2,1,0:T(8,128)S(1)} %get-tuple-element.41), channel_id=2, replica_groups=mesh['fac'=64,'chan'=4] {'chan'}, dimensions={0}, use_global_device_ids=true | all-gather | bytes 655360 | tf_op jit(solution)/shard_map/all_gather | solution.py:608
  125.5 0.0 copy-done.2
  125.5 1.9 %project.1 = f32[4,128,1024]{2,1,0:T(8,128)} custom-call(f32[4,128,1024]{2,1,0:T(8,128)S(1)} %get-tuple-element.40.update_ref, f32[4,8,1024]{2,1,0:T(8,128)S(1)} %copy-done.2, f32[4,4,8,1024]{3,2,1,0:T(8,128)S(1)} %bitcast.26), custom_call_target="tpu_custom_call" | custom-call | flops 4194304 | bytes 5242880 | tf_op jit(solution)/shard_map/project/pallas_call | solution.py:542
  (6 shorter events, 0.1 us)
Async XLA Ops:
  8.9 13.2 %copy-start.9 = (bf16[2,352,256]{2,1,0:T(8,128)(2,1)S(1)}, bf16[2,352,256]{2,1,0:T(8,128)(2,1)}, u32[]{:S(2)}) copy-start(bf16[2,352,256]{2,1,0:T(8,128)(2,1)} %constant.46.clone.rows_ref) | copy-start | bytes 1081348
  9.0 63.7 %all-to-all-start = ((f32[64,16,512]{2,1,0:T(8,128)}), f32[64,16,512]{2,1,0:T(8,128)S(1)}, u32[]{:S(2)}, u32[]{:S(2)}) async-start(f32[64,16,512]{2,1,0:T(8,128)} %bitcast.33), calls=%async_computation | async-start | bytes 4194304 | tf_op jit(solution)/shard_map/all_to_all | solution.py:574
  22.2 1.6 %copy-start = (f32[16,16,2048]{2,1,0:T(8,128)S(1)}, f32[16,16,2048]{2,1,0:T(8,128)}, u32[]{:S(2)}) copy-start(f32[16,16,2048]{2,1,0:T(8,128)} %param.16) | copy-start | bytes 6291460
  23.7 1.6 %copy-start.5 = (f32[4,16,8,1024]{3,2,1,0:T(8,128)S(1)}, f32[4,16,8,1024]{3,2,1,0:T(8,128)}, u32[]{:S(2)}) copy-start(f32[4,16,8,1024]{3,2,1,0:T(8,128)} %param.17) | copy-start | bytes 6291460
  25.3 1.1 copy-start.7
  31.7 1.0 copy-start.12
  32.7 1.0 copy-start.14
  33.7 45.5 %collective-permute-start = (f32[48,2048]{1,0:T(8,128)S(1)}, f32[48,2048]{1,0:T(8,128)S(1)}, u32[]{:S(2)}, u32[]{:S(2)}) collective-permute-start(f32[48,2048]{1,0:T(8,128)S(1)} %get-tuple-element.30), channel_id=1, source_target_pairs={{28,32},{60,64},{92,96},{124,128},{156,160},{188,192},{220,224},{2... | collective-permute-start | bytes 1179656 | tf_op jit(solution)/shard_map/ppermute | solution.py:582
  34.9 44.2 %collective-permute-start.1 = (f32[48,2048]{1,0:T(8,128)S(1)}, f32[48,2048]{1,0:T(8,128)}, u32[]{:S(2)}, u32[]{:S(2)}) collective-permute-start(f32[48,2048]{1,0:T(8,128)S(1)} %get-tuple-element.31), channel_id=1, source_target_pairs={{32,28},{64,60},{96,92},{128,124},{160,156},{192,188},{224,220},{3... | collective-permute-start | bytes 1179656 | tf_op jit(solution)/shard_map/ppermute | solution.py:582
  72.9 6.3 %copy-start.3 = (bf16[128,96]{1,0:T(8,128)(2,1)S(1)}, bf16[128,96]{1,0:T(8,128)(2,1)}, u32[]{:S(2)}) copy-start(bf16[128,96]{1,0:T(8,128)(2,1)} %constant.48.clone.place_ref) | copy-start | bytes 73732
  72.9 6.3 %copy-start.15 = (f32[128,2048]{1,0:T(8,128)S(1)}, f32[128,2048]{1,0:T(8,128)}, u32[]{:S(2)}) copy-start(f32[128,2048]{1,0:T(8,128)} %copy-done.14) | copy-start | bytes 3145732
  73.1 10.2 %collective-permute-start.2 = (f32[128,512]{1,0:T(8,128)S(1)}, f32[128,512]{1,0:T(8,128)S(1)}, u32[]{:S(2)}, u32[]{:S(2)}) collective-permute-start(f32[128,512]{1,0:T(8,128)S(1)} %get-tuple-element.27), channel_id=1, source_target_pairs={{0,1},{1,0},{2,3},{3,2},{4,5},{5,4},{6,7},{7,6},{8,9},{9,8},{10,11... | collective-permute-start | bytes 786440 | tf_op jit(solution)/shard_map/ppermute | solution.py:597
  73.2 12.9 %collective-permute-start.3 = (f32[128,512]{1,0:T(8,128)S(1)}, f32[128,512]{1,0:T(8,128)S(1)}, u32[]{:S(2)}, u32[]{:S(2)}) collective-permute-start(f32[128,512]{1,0:T(8,128)S(1)} %get-tuple-element.28), channel_id=1, source_target_pairs={{0,2},{1,3},{2,0},{3,1},{4,6},{5,7},{6,4},{7,5},{8,10},{9,11},{10,... | collective-permute-start | bytes 786440 | tf_op jit(solution)/shard_map/ppermute | solution.py:597
  76.0 15.5 %collective-permute-start.4 = (f32[128,512]{1,0:T(8,128)S(1)}, f32[128,512]{1,0:T(8,128)S(1)}, u32[]{:S(2)}, u32[]{:S(2)}) collective-permute-start(f32[128,512]{1,0:T(8,128)S(1)} %get-tuple-element.29), channel_id=1, source_target_pairs={{0,3},{1,2},{2,1},{3,0},{4,7},{5,6},{6,5},{7,4},{8,11},{9,10},{10,... | collective-permute-start | bytes 786440 | tf_op jit(solution)/shard_map/ppermute | solution.py:597
  79.1 2.8 %collective-permute-start.7 = (f32[2,128,512]{2,1,0:T(8,128)S(1)}, f32[2,128,512]{2,1,0:T(8,128)S(1)}, u32[]{:S(2)}, u32[]{:S(2)}) collective-permute-start(f32[2,128,512]{2,1,0:T(8,128)S(1)} %pad_maximum_fusion), channel_id=1, source_target_pairs={{0,1},{1,0},{2,3},{3,2},{4,5},{5,4},{6,7},{7,6},{8,9},{9,8},{10,11... | collective-permute-start | bytes 1572872 | tf_op jit(solution)/shard_map/ppermute | solution.py:598
  80.6 11.5 %collective-permute-start.5 = (f32[48,2048]{1,0:T(8,128)S(1)}, f32[48,2048]{1,0:T(8,128)S(1)}, u32[]{:S(2)}, u32[]{:S(2)}) collective-permute-start(f32[48,2048]{1,0:T(8,128)S(1)} %get-tuple-element.30), channel_id=1, source_target_pairs={{0,4},{4,8},{8,12},{12,16},{16,20},{20,24},{24,28},{32,36},{36,40}... | collective-permute-start | bytes 1179656 | tf_op jit(solution)/shard_map/ppermute | solution.py:584
  81.9 13.4 %collective-permute-start.6 = (f32[48,2048]{1,0:T(8,128)S(1)}, f32[48,2048]{1,0:T(8,128)S(1)}, u32[]{:S(2)}, u32[]{:S(2)}) collective-permute-start(f32[48,2048]{1,0:T(8,128)S(1)} %get-tuple-element.31), channel_id=1, source_target_pairs={{4,0},{8,4},{12,8},{16,12},{20,16},{24,20},{28,24},{36,32},{40,36}... | collective-permute-start | bytes 1179656 | tf_op jit(solution)/shard_map/ppermute | solution.py:584
  83.3 22.5 %collective-permute-start.8 = (f32[2,128,512]{2,1,0:T(8,128)S(1)}, f32[2,128,512]{2,1,0:T(8,128)S(1)}, u32[]{:S(2)}, u32[]{:S(2)}) collective-permute-start(f32[2,128,512]{2,1,0:T(8,128)S(1)} %pad_maximum_fusion.1), channel_id=1, source_target_pairs={{0,2},{1,3},{2,0},{3,1},{4,6},{5,7},{6,4},{7,5},{8,10},{9,11},{10,... | collective-permute-start | bytes 1572872 | tf_op jit(solution)/shard_map/ppermute | solution.py:599
  91.5 3.8 %copy-start.1 = (f32[16,16,2048]{2,1,0:T(8,128)S(1)}, f32[16,16,2048]{2,1,0:T(8,128)}, u32[]{:S(2)}) copy-start(f32[16,16,2048]{2,1,0:T(8,128)} %param.16) | copy-start | bytes 6291460
  91.5 3.8 %copy-start.4 = (bf16[96,128]{1,0:T(8,128)(2,1)S(1)}, bf16[96,128]{1,0:T(8,128)(2,1)}, u32[]{:S(2)}) copy-start(bf16[96,128]{1,0:T(8,128)(2,1)} %constant.49.clone.pick_ref) | copy-start | bytes 73732
  92.0 13.8 %copy-start.6 = (f32[4,16,8,1024]{3,2,1,0:T(8,128)S(1)}, f32[4,16,8,1024]{3,2,1,0:T(8,128)}, u32[]{:S(2)}) copy-start(f32[4,16,8,1024]{3,2,1,0:T(8,128)} %param.17) | copy-start | bytes 6291460
  92.0 13.8 %copy-start.8 = (bf16[2,512,256]{2,1,0:T(8,128)(2,1)S(1)}, bf16[2,512,256]{2,1,0:T(8,128)(2,1)}, u32[]{:S(2)}) copy-start(bf16[2,512,256]{2,1,0:T(8,128)(2,1)} %constant.51.clone.columns_ref) | copy-start | bytes 1572868
  92.1 13.8 %copy-start.10 = (bf16[2,256,256]{2,1,0:T(8,128)(2,1)S(1)}, bf16[2,256,256]{2,1,0:T(8,128)(2,1)}, u32[]{:S(2)}) copy-start(bf16[2,256,256]{2,1,0:T(8,128)(2,1)} %constant.50.clone.rows_ref) | copy-start | bytes 786436
  92.1 13.8 %copy-start.13 = (f32[128,2048]{1,0:T(8,128)S(1)}, f32[128,2048]{1,0:T(8,128)}, u32[]{:S(2)}) copy-start(f32[128,2048]{1,0:T(8,128)} %copy-done.12) | copy-start | bytes 3145732
  97.0 15.6 %collective-permute-start.9 = (f32[48,2048]{1,0:T(8,128)S(1)}, f32[48,2048]{1,0:T(8,128)S(1)}, u32[]{:S(2)}, u32[]{:S(2)}) collective-permute-start(f32[48,2048]{1,0:T(8,128)S(1)} %get-tuple-element.38), channel_id=1, source_target_pairs={{0,4},{4,8},{8,12},{12,16},{16,20},{20,24},{24,28},{28,32},{32,36}... | collective-permute-start | bytes 1179656 | tf_op jit(solution)/shard_map/ppermute | solution.py:604
  98.9 14.9 %collective-permute-start.10 = (f32[48,2048]{1,0:T(8,128)S(1)}, f32[48,2048]{1,0:T(8,128)S(1)}, u32[]{:S(2)}, u32[]{:S(2)}) collective-permute-start(f32[48,2048]{1,0:T(8,128)S(1)} %get-tuple-element.39), channel_id=1, source_target_pairs={{4,0},{8,4},{12,8},{16,12},{20,16},{24,20},{28,24},{32,28},{36,32}... | collective-permute-start | bytes 1179656 | tf_op jit(solution)/shard_map/ppermute | solution.py:605
  105.9 7.9 %copy-start.11 = (bf16[2,256,96]{2,1,0:T(8,128)(2,1)S(1)}, bf16[2,256,96]{2,1,0:T(8,128)(2,1)}, u32[]{:S(2)}) copy-start(bf16[2,256,96]{2,1,0:T(8,128)(2,1)} %constant.52.clone.rows_ref) | copy-start | bytes 294916
  113.8 11.7 %copy-start.2 = (f32[4,8,1024]{2,1,0:T(8,128)S(1)}, f32[4,8,1024]{2,1,0:T(8,128)}, u32[]{:S(2)}) copy-start(f32[4,8,1024]{2,1,0:T(8,128)} %weight_ref.1) | copy-start | bytes 393220

commit v4 on v3

--- a/solution.py
+++ b/solution.py
@@ -526,26 +526,27 @@
 
 
 def project_kernel(update_ref, weight_ref, sums_ref, out_ref):
-    total = (sums_ref[0, 0] + sums_ref[1, 0]) + (sums_ref[2, 0] + sums_ref[3, 0])
-    weight = weight_ref[0]
+    total = (sums_ref[0] + sums_ref[1]) + (sums_ref[2] + sums_ref[3])
+    weight = weight_ref[...]
     factor = weight / jnp.maximum(jnp.sqrt(total), weight)
-    count = factor.shape[0]
+    count = factor.shape[1]
     for channel in range(update_ref.shape[1] // count):
         rows = slice(channel * count, (channel + 1) * count)
-        out_ref[0, rows, :] = update_ref[0, rows, :] * factor
+        out_ref[:, rows, :] = update_ref[:, rows, :] * factor
 
 
 def project(update, weight, sums):
     bands, pixels, columns = update.shape
     half = weight.shape[1]
-    wide = pl.BlockSpec((1, pixels, columns), lambda i: (i, 0, 0))
+    each = 2
+    wide = pl.BlockSpec((each, pixels, columns), lambda i: (i, 0, 0))
     return pl.pallas_call(
         project_kernel,
-        grid=(bands,),
+        grid=(bands // each,),
         in_specs=[
             wide,
-            pl.BlockSpec((1, half, columns), lambda i: (i, 0, 0)),
-            pl.BlockSpec((sums.shape[0], 1, half, columns), lambda i: (0, i, 0, 0)),
+            pl.BlockSpec((each, half, columns), lambda i: (i, 0, 0)),
+            pl.BlockSpec((sums.shape[0], each, half, columns), lambda i: (0, i, 0, 0)),
         ],
         out_specs=wide,
         out_shape=jax.ShapeDtypeStruct(update.shape, jnp.float32),

time: 129 us -> 128 us (level)
  no operation moved by 1% of the time
where the time goes in v4:
time: 128 us; the launch traced here: 127 us
  waiting for transfers between devices  42.3 us (33%)
  starting transfers between devices  40.5 us (32%)
  Pallas kernels  28 us (22%)
  blocking collectives  8.41 us (7%)
  local copies, waits for them, and re-layouts  6.7 us (5%)
    all_to_all x1, waiting for transfers between devices, shards(): lax.all_to_all(grid.reshape(facets, rows, quarter), 'fac', split_axis=0,...  29.4 us
    all_to_all x1, starting transfers between devices, shards(): lax.all_to_all(grid.reshape(facets, rows, quarter), 'fac', split_axis=0,...  13.2 us
    all_gather x1, blocking collectives, shards(): sums = lax.all_gather(squares, 'chan')  8.41 us
    ppermute x1, starting transfers between devices, shards(): lax.ppermute(to_above, 'fac', turned(far))  8.35 us
    pallas_call x1, Pallas kernels, back_project(): pl.pallas_call(functools.partial(back_kernel, rows=rows), in_specs=[vmem,...  8.3 us
    ppermute x1, starting transfers between devices, shards(): below = lax.ppermute(first, 'fac', backward)  6.93 us
    unnamed x32, local copies, waits for them, and re-layouts  6.32 us
    pallas_call x1, Pallas kernels, finish(): pl.pallas_call(finish_kernel, grid_spec=pltpu.PrefetchScalarGridSpec(num_...  6.23 us
  transfers between devices with their start and end apart: 12, of which 6 were waited for; matrix products, arithmetic and copies ran while one was open for 0% of the time, Pallas kernels for 12%

profile of v4, /device:TPU:8, one launch (start us, length us, event | category | flops | bytes accessed | tf_op | source)
XLA Modules:
  0.0 127.0 jit_solution(9217311107042280851)
XLA Ops:
  0.6 8.3 %back_project.1 = f32[1024,512]{1,0:T(8,128)} custom-call(bf16[1,4096]{1,0:T(2,128)(2,1)} %vis_ref.1, s32[1,4096]{1,0:T(1,128)} %tile_ref.1, bf16[4096,128]{1,0:T(8,128)(2,1)} %bitcast.36, s32[4096,128]{1,0:T(8,128)} %bitcast.35), custom_call_target="tpu_custom_call" | custom-call | flops 4294967296 | bytes 6291456 | tf_op jit(solution)/shard_map/back_project/pallas_call | solution.py:183
  8.9 0.0 copy-start.9
  9.0 13.2 %all-to-all-start = ((f32[64,16,512]{2,1,0:T(8,128)}), f32[64,16,512]{2,1,0:T(8,128)S(1)}, u32[]{:S(2)}, u32[]{:S(2)}) async-start(f32[64,16,512]{2,1,0:T(8,128)} %bitcast.33), calls=%async_computation | async-start | bytes 4194304 | tf_op jit(solution)/shard_map/all_to_all | solution.py:575
  22.1 0.0 copy-done.9
  22.2 0.0 copy-start
  22.2 1.6 %copy-done = f32[16,16,2048]{2,1,0:T(8,128)S(1)} copy-done((f32[16,16,2048]{2,1,0:T(8,128)S(1)}, f32[16,16,2048]{2,1,0:T(8,128)}, u32[]{:S(2)}) %copy-start) | copy-done | bytes 2097176
  23.7 0.0 copy-start.5
  23.8 1.6 %copy-done.5 = f32[4,16,8,1024]{3,2,1,0:T(8,128)S(1)} copy-done((f32[4,16,8,1024]{3,2,1,0:T(8,128)S(1)}, f32[4,16,8,1024]{3,2,1,0:T(8,128)}, u32[]{:S(2)}) %copy-start.5) | copy-done | bytes 2097176
  25.3 0.0 copy-start.7
  25.3 1.1 copy-done.7
  26.5 5.2 %synthesis.1 = (f32[128,2048]{1,0:T(8,128)S(1)}, f32[128,2048]{1,0:T(8,128)S(1)}, f32[48,2048]{1,0:T(8,128)S(1)}, f32[48,2048]{1,0:T(8,128)S(1)}) custom-call(f32[4,128,1024]{2,1,0:T(8,128)S(1)} %bitcast.30, f32[16,2,8,2048]{3,2,1,0:T(8,128)S(1)} %bitcast.27, bf16[2,352,256]{2,1,0:T(8,128)(2,1)S(1)} %copy-done.9, bf16[2,768,256]{2,1,0:T(8,128)(2,1)S(1)} %copy-done.7), custom_call_target="tpu_custom_call" | custom-call | flops 8589934592 | bytes 8388608 | tf_op jit(solution)/shard_map/synthesis/pallas_call | solution.py:245
  31.7 0.0 copy-start.12
  31.7 1.0 copy-done.12
  32.7 0.0 copy-start.14
  32.7 1.0 copy-done.14
  33.7 1.3 %collective-permute-start = (f32[48,2048]{1,0:T(8,128)S(1)}, f32[48,2048]{1,0:T(8,128)S(1)}, u32[]{:S(2)}, u32[]{:S(2)}) collective-permute-start(f32[48,2048]{1,0:T(8,128)S(1)} %get-tuple-element.30), channel_id=1, source_target_pairs={{28,32},{60,64},{92,96},{124,128},{156,160},{188,192},{220,224},{2... | collective-permute-start | bytes 1179656 | tf_op jit(solution)/shard_map/ppermute | solution.py:583
  34.9 8.3 %collective-permute-start.1 = (f32[48,2048]{1,0:T(8,128)S(1)}, f32[48,2048]{1,0:T(8,128)}, u32[]{:S(2)}, u32[]{:S(2)}) collective-permute-start(f32[48,2048]{1,0:T(8,128)S(1)} %get-tuple-element.31), channel_id=1, source_target_pairs={{32,28},{64,60},{96,92},{128,124},{160,156},{192,188},{224,220},{3... | collective-permute-start | bytes 1179656 | tf_op jit(solution)/shard_map/ppermute | solution.py:583
  43.3 29.4 %all-to-all-done = f32[64,16,512]{2,1,0:T(8,128)S(1)} async-done(((f32[64,16,512]{2,1,0:T(8,128)}), f32[64,16,512]{2,1,0:T(8,128)S(1)}, u32[]{:S(2)}, u32[]{:S(2)}) %all-to-all-start) | async-done | bytes 2097184 | tf_op jit(solution)/shard_map/all_to_all | solution.py:575
  72.7 0.2 fusion
  72.9 0.0 copy-start.3
  72.9 0.0 copy-start.15
  72.9 0.2 dynamic-slice_bitcast_fusion
  73.1 0.1 collective-permute-start.2
  73.2 2.8 %collective-permute-start.3 = (f32[128,512]{1,0:T(8,128)S(1)}, f32[128,512]{1,0:T(8,128)S(1)}, u32[]{:S(2)}, u32[]{:S(2)}) collective-permute-start(f32[128,512]{1,0:T(8,128)S(1)} %get-tuple-element.28), channel_id=1, source_target_pairs={{0,2},{1,3},{2,0},{3,1},{4,6},{5,7},{6,4},{7,5},{8,10},{9,11},{10,... | collective-permute-start | bytes 786440 | tf_op jit(solution)/shard_map/ppermute | solution.py:598
  76.0 0.6 collective-permute-start.4
  76.6 2.6 %collective-permute-done.above_ref = f32[48,2048]{1,0:T(8,128)S(1)} collective-permute-done((f32[48,2048]{1,0:T(8,128)S(1)}, f32[48,2048]{1,0:T(8,128)S(1)}, u32[]{:S(2)}, u32[]{:S(2)}) %collective-permute-start) | collective-permute-done | bytes 393248 | tf_op jit(solution)/shard_map/ppermute | solution.py:583
  79.1 0.0 collective-permute-start.7
  79.2 0.0 collective-permute-done.1.below_ref
  79.2 0.0 copy-done.3
  79.2 0.0 copy-done.15
  79.2 1.4 %add_sides.1.base_ref = f32[128,2048]{1,0:T(8,128)S(1)} custom-call(f32[128,2048]{1,0:T(8,128)S(1)} %copy-done.15, f32[48,2048]{1,0:T(8,128)S(1)} %collective-permute-done.above_ref, f32[48,2048]{1,0:T(8,128)} %collective-permute-done.1.below_ref, bf16[128,96]{1,0:T(8,128)(2,1)S(1)} %copy-done.3), custom_call_target="tpu_custom_call" | custom-call | flops 42949672960 | bytes 3145728 | tf_op jit(solution)/shard_map/add_sides/pallas_call | solution.py:270
  80.6 1.3 %collective-permute-start.5 = (f32[48,2048]{1,0:T(8,128)S(1)}, f32[48,2048]{1,0:T(8,128)S(1)}, u32[]{:S(2)}, u32[]{:S(2)}) collective-permute-start(f32[48,2048]{1,0:T(8,128)S(1)} %get-tuple-element.30), channel_id=1, source_target_pairs={{0,4},{4,8},{8,12},{12,16},{16,20},{20,24},{24,28},{32,36},{36,40}... | collective-permute-start | bytes 1179656 | tf_op jit(solution)/shard_map/ppermute | solution.py:585
  81.9 0.0 collective-permute-done.7.one_ref
  81.9 1.3 %collective-permute-start.6 = (f32[48,2048]{1,0:T(8,128)S(1)}, f32[48,2048]{1,0:T(8,128)S(1)}, u32[]{:S(2)}, u32[]{:S(2)}) collective-permute-start(f32[48,2048]{1,0:T(8,128)S(1)} %get-tuple-element.31), channel_id=1, source_target_pairs={{4,0},{8,4},{12,8},{16,12},{20,16},{24,20},{28,24},{36,32},{40,36}... | collective-permute-start | bytes 1179656 | tf_op jit(solution)/shard_map/ppermute | solution.py:585
  83.3 0.0 collective-permute-done.2.one_ref
  83.3 2.8 %collective-permute-start.8 = (f32[2,128,512]{2,1,0:T(8,128)S(1)}, f32[2,128,512]{2,1,0:T(8,128)S(1)}, u32[]{:S(2)}, u32[]{:S(2)}) collective-permute-start(f32[2,128,512]{2,1,0:T(8,128)S(1)} %pad_maximum_fusion.1), channel_id=1, source_target_pairs={{0,2},{1,3},{2,0},{3,1},{4,6},{5,7},{6,4},{7,5},{8,10},{9,11},{10,... | collective-permute-start | bytes 1572872 | tf_op jit(solution)/shard_map/ppermute | solution.py:600
  86.1 0.0 collective-permute-done.3.two_ref
  86.1 5.4 %collective-permute-done.4.three_ref = f32[128,512]{1,0:T(8,128)S(1)} collective-permute-done((f32[128,512]{1,0:T(8,128)S(1)}, f32[128,512]{1,0:T(8,128)S(1)}, u32[]{:S(2)}, u32[]{:S(2)}) %collective-permute-start.4) | collective-permute-done | bytes 262176 | tf_op jit(solution)/shard_map/ppermute | solution.py:598
  91.5 0.5 border_sum.1.base_ref
  92.0 0.0 copy-start.6
  92.0 0.0 copy-start.8
  92.1 0.0 copy-start.10
  92.1 0.0 copy-start.13
  92.1 0.0 collective-permute-done.5.above_ref
  92.1 3.3 %collective-permute-done.6.below_ref = f32[48,2048]{1,0:T(8,128)S(1)} collective-permute-done((f32[48,2048]{1,0:T(8,128)S(1)}, f32[48,2048]{1,0:T(8,128)S(1)}, u32[]{:S(2)}, u32[]{:S(2)}) %collective-permute-start.6) | collective-permute-done | bytes 393248 | tf_op jit(solution)/shard_map/ppermute | solution.py:585
  95.3 0.0 copy-done.1
  95.4 0.0 copy-done.4
  95.4 1.6 %update_border.1 = (f32[128,2048]{1,0:T(8,128)S(1)}, f32[48,2048]{1,0:T(8,128)S(1)}, f32[48,2048]{1,0:T(8,128)S(1)}) custom-call(f32[128,2048]{1,0:T(8,128)S(1)} %border_sum.1.base_ref, f32[48,2048]{1,0:T(8,128)S(1)} %collective-permute-done.5.above_ref, f32[48,2048]{1,0:T(8,128)S(1)} %collective-permute-done.6.below_ref, f32[16,2,8,2048]{3,2,1,0:T(8,128)S(1)} %bitcast.28, ...), custom_call_target="tpu_custom_call" | custom-call | flops 4194304 | bytes 4194304 | tf_op jit(solution)/shard_map/update_border/pallas_call | solution.py:333
  97.0 1.9 %collective-permute-start.9 = (f32[48,2048]{1,0:T(8,128)S(1)}, f32[48,2048]{1,0:T(8,128)S(1)}, u32[]{:S(2)}, u32[]{:S(2)}) collective-permute-start(f32[48,2048]{1,0:T(8,128)S(1)} %get-tuple-element.38), channel_id=1, source_target_pairs={{0,4},{4,8},{8,12},{12,16},{16,20},{20,24},{24,28},{28,32},{32,36}... | collective-permute-start | bytes 1179656 | tf_op jit(solution)/shard_map/ppermute | solution.py:605
  98.9 6.9 %collective-permute-start.10 = (f32[48,2048]{1,0:T(8,128)S(1)}, f32[48,2048]{1,0:T(8,128)S(1)}, u32[]{:S(2)}, u32[]{:S(2)}) collective-permute-start(f32[48,2048]{1,0:T(8,128)S(1)} %get-tuple-element.39), channel_id=1, source_target_pairs={{4,0},{8,4},{12,8},{16,12},{20,16},{24,20},{28,24},{32,28},{36,32}... | collective-permute-start | bytes 1179656 | tf_op jit(solution)/shard_map/ppermute | solution.py:606
  105.8 0.0 collective-permute-done.8.two_ref.three_ref
  105.8 0.0 copy-done.6
  105.9 0.0 copy-done.8
  105.9 0.0 copy-done.10
  105.9 0.0 copy-done.13
  105.9 0.0 copy-start.11
  105.9 6.2 %finish.1 = (f32[16,2,8,2048]{3,2,1,0:T(8,128)}, f32[4,128,1024]{2,1,0:T(8,128)S(1)}) custom-call(s32[1]{0:T(128)} %bitcast.me_ref, f32[128,2048]{1,0:T(8,128)S(1)} %get-tuple-element.32.image_a_ref, f32[128,2048]{1,0:T(8,128)S(1)} %copy-done.13, f32[4,16,2,8,512]{4,3,2,1,0:T(8,128)S(1)} %bitcast.25, f32[2,128,512]{2,1,0:T(8,128)S(1)} %collective-permute-done.7.one_ref, ...), custom_call_target="tpu_custom_call" | custom-call | flops 4294967296 | bytes 12582912 | tf_op jit(solution)/shard_map/finish/pallas_call | solution.py:425
  112.1 0.5 collective-permute-done.9.above_ref
  112.6 1.2 collective-permute-done.10.below_ref
  113.8 0.0 copy-done.11
  113.8 3.3 %add_halo.1 = (f32[4,128,1024]{2,1,0:T(8,128)S(1)}, f32[4,8,1024]{2,1,0:T(8,128)S(1)}) custom-call(f32[4,128,1024]{2,1,0:T(8,128)S(1)} %get-tuple-element.37.main_ref, f32[48,2048]{1,0:T(8,128)S(1)} %collective-permute-done.9.above_ref, f32[48,2048]{1,0:T(8,128)S(1)} %collective-permute-done.10.below_ref, bf16[2,256,96]{2,1,0:T(8,128)(2,1)S(1)} %copy-done.11, ...), custom_call_target="tpu_custom_call" | custom-call | flops 1073741824 | bytes 5242880 | tf_op jit(solution)/shard_map/add_halo/pallas_call | solution.py:506
  117.1 8.4 %all-gather = f32[16,8,1024]{2,1,0:T(8,128)S(1)} all-gather(f32[4,8,1024]{2,1,0:T(8,128)S(1)} %get-tuple-element.41), channel_id=2, replica_groups=mesh['fac'=64,'chan'=4] {'chan'}, dimensions={0}, use_global_device_ids=true | all-gather | bytes 655360 | tf_op jit(solution)/shard_map/all_gather | solution.py:609
  125.5 0.0 copy-done.2
  125.5 1.5 %project.1 = f32[4,128,1024]{2,1,0:T(8,128)} custom-call(f32[4,128,1024]{2,1,0:T(8,128)S(1)} %get-tuple-element.40.update_ref, f32[4,8,1024]{2,1,0:T(8,128)S(1)} %copy-done.2, f32[4,4,8,1024]{3,2,1,0:T(8,128)S(1)} %bitcast.26), custom_call_target="tpu_custom_call" | custom-call | flops 4194304 | bytes 5242880 | tf_op jit(solution)/shard_map/project/pallas_call | solution.py:543
  (6 shorter events, 0.1 us)
Async XLA Ops:
  8.9 13.2 %copy-start.9 = (bf16[2,352,256]{2,1,0:T(8,128)(2,1)S(1)}, bf16[2,352,256]{2,1,0:T(8,128)(2,1)}, u32[]{:S(2)}) copy-start(bf16[2,352,256]{2,1,0:T(8,128)(2,1)} %constant.46.clone.rows_ref) | copy-start | bytes 1081348
  9.0 63.7 %all-to-all-start = ((f32[64,16,512]{2,1,0:T(8,128)}), f32[64,16,512]{2,1,0:T(8,128)S(1)}, u32[]{:S(2)}, u32[]{:S(2)}) async-start(f32[64,16,512]{2,1,0:T(8,128)} %bitcast.33), calls=%async_computation | async-start | bytes 4194304 | tf_op jit(solution)/shard_map/all_to_all | solution.py:575
  22.2 1.6 %copy-start = (f32[16,16,2048]{2,1,0:T(8,128)S(1)}, f32[16,16,2048]{2,1,0:T(8,128)}, u32[]{:S(2)}) copy-start(f32[16,16,2048]{2,1,0:T(8,128)} %param.16) | copy-start | bytes 6291460
  23.7 1.6 %copy-start.5 = (f32[4,16,8,1024]{3,2,1,0:T(8,128)S(1)}, f32[4,16,8,1024]{3,2,1,0:T(8,128)}, u32[]{:S(2)}) copy-start(f32[4,16,8,1024]{3,2,1,0:T(8,128)} %param.17) | copy-start | bytes 6291460
  25.3 1.1 copy-start.7
  31.7 1.0 copy-start.12
  32.7 1.0 copy-start.14
  33.7 45.5 %collective-permute-start = (f32[48,2048]{1,0:T(8,128)S(1)}, f32[48,2048]{1,0:T(8,128)S(1)}, u32[]{:S(2)}, u32[]{:S(2)}) collective-permute-start(f32[48,2048]{1,0:T(8,128)S(1)} %get-tuple-element.30), channel_id=1, source_target_pairs={{28,32},{60,64},{92,96},{124,128},{156,160},{188,192},{220,224},{2... | collective-permute-start | bytes 1179656 | tf_op jit(solution)/shard_map/ppermute | solution.py:583
  34.9 44.2 %collective-permute-start.1 = (f32[48,2048]{1,0:T(8,128)S(1)}, f32[48,2048]{1,0:T(8,128)}, u32[]{:S(2)}, u32[]{:S(2)}) collective-permute-start(f32[48,2048]{1,0:T(8,128)S(1)} %get-tuple-element.31), channel_id=1, source_target_pairs={{32,28},{64,60},{96,92},{128,124},{160,156},{192,188},{224,220},{3... | collective-permute-start | bytes 1179656 | tf_op jit(solution)/shard_map/ppermute | solution.py:583
  72.9 6.3 %copy-start.3 = (bf16[128,96]{1,0:T(8,128)(2,1)S(1)}, bf16[128,96]{1,0:T(8,128)(2,1)}, u32[]{:S(2)}) copy-start(bf16[128,96]{1,0:T(8,128)(2,1)} %constant.48.clone.place_ref) | copy-start | bytes 73732
  72.9 6.3 %copy-start.15 = (f32[128,2048]{1,0:T(8,128)S(1)}, f32[128,2048]{1,0:T(8,128)}, u32[]{:S(2)}) copy-start(f32[128,2048]{1,0:T(8,128)} %copy-done.14) | copy-start | bytes 3145732
  73.1 10.2 %collective-permute-start.2 = (f32[128,512]{1,0:T(8,128)S(1)}, f32[128,512]{1,0:T(8,128)S(1)}, u32[]{:S(2)}, u32[]{:S(2)}) collective-permute-start(f32[128,512]{1,0:T(8,128)S(1)} %get-tuple-element.27), channel_id=1, source_target_pairs={{0,1},{1,0},{2,3},{3,2},{4,5},{5,4},{6,7},{7,6},{8,9},{9,8},{10,11... | collective-permute-start | bytes 786440 | tf_op jit(solution)/shard_map/ppermute | solution.py:598
  73.2 12.9 %collective-permute-start.3 = (f32[128,512]{1,0:T(8,128)S(1)}, f32[128,512]{1,0:T(8,128)S(1)}, u32[]{:S(2)}, u32[]{:S(2)}) collective-permute-start(f32[128,512]{1,0:T(8,128)S(1)} %get-tuple-element.28), channel_id=1, source_target_pairs={{0,2},{1,3},{2,0},{3,1},{4,6},{5,7},{6,4},{7,5},{8,10},{9,11},{10,... | collective-permute-start | bytes 786440 | tf_op jit(solution)/shard_map/ppermute | solution.py:598
  76.0 15.5 %collective-permute-start.4 = (f32[128,512]{1,0:T(8,128)S(1)}, f32[128,512]{1,0:T(8,128)S(1)}, u32[]{:S(2)}, u32[]{:S(2)}) collective-permute-start(f32[128,512]{1,0:T(8,128)S(1)} %get-tuple-element.29), channel_id=1, source_target_pairs={{0,3},{1,2},{2,1},{3,0},{4,7},{5,6},{6,5},{7,4},{8,11},{9,10},{10,... | collective-permute-start | bytes 786440 | tf_op jit(solution)/shard_map/ppermute | solution.py:598
  79.1 2.8 %collective-permute-start.7 = (f32[2,128,512]{2,1,0:T(8,128)S(1)}, f32[2,128,512]{2,1,0:T(8,128)S(1)}, u32[]{:S(2)}, u32[]{:S(2)}) collective-permute-start(f32[2,128,512]{2,1,0:T(8,128)S(1)} %pad_maximum_fusion), channel_id=1, source_target_pairs={{0,1},{1,0},{2,3},{3,2},{4,5},{5,4},{6,7},{7,6},{8,9},{9,8},{10,11... | collective-permute-start | bytes 1572872 | tf_op jit(solution)/shard_map/ppermute | solution.py:599
  80.6 11.5 %collective-permute-start.5 = (f32[48,2048]{1,0:T(8,128)S(1)}, f32[48,2048]{1,0:T(8,128)S(1)}, u32[]{:S(2)}, u32[]{:S(2)}) collective-permute-start(f32[48,2048]{1,0:T(8,128)S(1)} %get-tuple-element.30), channel_id=1, source_target_pairs={{0,4},{4,8},{8,12},{12,16},{16,20},{20,24},{24,28},{32,36},{36,40}... | collective-permute-start | bytes 1179656 | tf_op jit(solution)/shard_map/ppermute | solution.py:585
  81.9 13.4 %collective-permute-start.6 = (f32[48,2048]{1,0:T(8,128)S(1)}, f32[48,2048]{1,0:T(8,128)S(1)}, u32[]{:S(2)}, u32[]{:S(2)}) collective-permute-start(f32[48,2048]{1,0:T(8,128)S(1)} %get-tuple-element.31), channel_id=1, source_target_pairs={{4,0},{8,4},{12,8},{16,12},{20,16},{24,20},{28,24},{36,32},{40,36}... | collective-permute-start | bytes 1179656 | tf_op jit(solution)/shard_map/ppermute | solution.py:585
  83.3 22.5 %collective-permute-start.8 = (f32[2,128,512]{2,1,0:T(8,128)S(1)}, f32[2,128,512]{2,1,0:T(8,128)S(1)}, u32[]{:S(2)}, u32[]{:S(2)}) collective-permute-start(f32[2,128,512]{2,1,0:T(8,128)S(1)} %pad_maximum_fusion.1), channel_id=1, source_target_pairs={{0,2},{1,3},{2,0},{3,1},{4,6},{5,7},{6,4},{7,5},{8,10},{9,11},{10,... | collective-permute-start | bytes 1572872 | tf_op jit(solution)/shard_map/ppermute | solution.py:600
  91.5 3.8 %copy-start.1 = (f32[16,16,2048]{2,1,0:T(8,128)S(1)}, f32[16,16,2048]{2,1,0:T(8,128)}, u32[]{:S(2)}) copy-start(f32[16,16,2048]{2,1,0:T(8,128)} %param.16) | copy-start | bytes 6291460
  91.5 3.8 %copy-start.4 = (bf16[96,128]{1,0:T(8,128)(2,1)S(1)}, bf16[96,128]{1,0:T(8,128)(2,1)}, u32[]{:S(2)}) copy-start(bf16[96,128]{1,0:T(8,128)(2,1)} %constant.49.clone.pick_ref) | copy-start | bytes 73732
  92.0 13.8 %copy-start.6 = (f32[4,16,8,1024]{3,2,1,0:T(8,128)S(1)}, f32[4,16,8,1024]{3,2,1,0:T(8,128)}, u32[]{:S(2)}) copy-start(f32[4,16,8,1024]{3,2,1,0:T(8,128)} %param.17) | copy-start | bytes 6291460
  92.0 13.8 %copy-start.8 = (bf16[2,512,256]{2,1,0:T(8,128)(2,1)S(1)}, bf16[2,512,256]{2,1,0:T(8,128)(2,1)}, u32[]{:S(2)}) copy-start(bf16[2,512,256]{2,1,0:T(8,128)(2,1)} %constant.51.clone.columns_ref) | copy-start | bytes 1572868
  92.1 13.8 %copy-start.10 = (bf16[2,256,256]{2,1,0:T(8,128)(2,1)S(1)}, bf16[2,256,256]{2,1,0:T(8,128)(2,1)}, u32[]{:S(2)}) copy-start(bf16[2,256,256]{2,1,0:T(8,128)(2,1)} %constant.50.clone.rows_ref) | copy-start | bytes 786436
  92.1 13.8 %copy-start.13 = (f32[128,2048]{1,0:T(8,128)S(1)}, f32[128,2048]{1,0:T(8,128)}, u32[]{:S(2)}) copy-start(f32[128,2048]{1,0:T(8,128)} %copy-done.12) | copy-start | bytes 3145732
  97.0 15.6 %collective-permute-start.9 = (f32[48,2048]{1,0:T(8,128)S(1)}, f32[48,2048]{1,0:T(8,128)S(1)}, u32[]{:S(2)}, u32[]{:S(2)}) collective-permute-start(f32[48,2048]{1,0:T(8,128)S(1)} %get-tuple-element.38), channel_id=1, source_target_pairs={{0,4},{4,8},{8,12},{12,16},{16,20},{20,24},{24,28},{28,32},{32,36}... | collective-permute-start | bytes 1179656 | tf_op jit(solution)/shard_map/ppermute | solution.py:605
  98.9 14.9 %collective-permute-start.10 = (f32[48,2048]{1,0:T(8,128)S(1)}, f32[48,2048]{1,0:T(8,128)S(1)}, u32[]{:S(2)}, u32[]{:S(2)}) collective-permute-start(f32[48,2048]{1,0:T(8,128)S(1)} %get-tuple-element.39), channel_id=1, source_target_pairs={{4,0},{8,4},{12,8},{16,12},{20,16},{24,20},{28,24},{32,28},{36,32}... | collective-permute-start | bytes 1179656 | tf_op jit(solution)/shard_map/ppermute | solution.py:606
  105.9 7.9 %copy-start.11 = (bf16[2,256,96]{2,1,0:T(8,128)(2,1)S(1)}, bf16[2,256,96]{2,1,0:T(8,128)(2,1)}, u32[]{:S(2)}) copy-start(bf16[2,256,96]{2,1,0:T(8,128)(2,1)} %constant.52.clone.rows_ref) | copy-start | bytes 294916
  113.8 11.7 %copy-start.2 = (f32[4,8,1024]{2,1,0:T(8,128)S(1)}, f32[4,8,1024]{2,1,0:T(8,128)}, u32[]{:S(2)}) copy-start(f32[4,8,1024]{2,1,0:T(8,128)} %weight_ref.1) | copy-start | bytes 393220
